TPU v7x, 32 devices: a whole 2x2x4 slice. The times are simulated.
32 devices in a mesh: ctx: 8 (over z, y), head: 4 (over x, core).
Axes of the slice: x: 2, y: 2, z: 4, core: 2. Of those that a mesh axis runs over, the one named last changes fastest.
Arguments:
- tokens: bfloat16 [4096, 1024], P(('ctx', 'head')), may hold values from -6 to 6
- conv_kernel: float32 [7, 1024], replicated, may hold values from -2.5 to 2.5
- w_qkv: bfloat16 [1024, 3072], replicated, may hold values from -0.1875 to 0.1875
- w_out: bfloat16 [1024, 1024], replicated, may hold values from -0.1875 to 0.1875
- lengths: int32 [4], replicated, may hold values from 1 to 2048, 4096 in all
- cotangent: bfloat16 [4096, 1024], P(('ctx', 'head')), may hold values from -6 to 6
Outputs:
- attended: bfloat16 [4096, 1024], P(('ctx', 'head'))
- input_grad: bfloat16 [4096, 1024], P(('ctx', 'head'))
Inputs may be any that keep to these rules, and one draw needn't show every extreme that they name: `lengths`: they sum to 4096; the longest recording has exactly 2048 tokens.
All inputs are finite; a program needn't handle non-finite values.
Results may differ from a plain program's by a relative error of at most 0.017.
The roundings to bfloat16 on the way count: a program that leaves them out, or rounds other values in their place, can miss the bound.
Values may be sent and summed in bfloat16 or wider, within the bound.
No kernel may reach another device: no remote copies, remote signals or barrier semaphores. Data moves between devices by JAX's collectives and lax.ppermute only.
A program may use at most 128 MiB of HBM per device.

v0:
```python
import functools
import math

import jax
import jax.numpy as jnp
from jax import lax
from jax.experimental import pallas as pl
from jax.experimental.pallas import tpu as pltpu
from jax.sharding import PartitionSpec as P

HD = 64
KS = 7
HALF = KS // 2
MAXLEN = 2048
AXES = ("ctx", "head")
LANES = 128
EDGE = 16
PER_STEP = 2
FAR = -1e30
FRONT_STEPS = 4
BACK_STEPS = 4
VMEM_ALL = 60 * 1024 * 1024
VMEM_MOST = 44 * 1024 * 1024
VMEM_SOME = 24 * 1024 * 1024
F32 = jnp.float32
BF16 = jnp.bfloat16


def params(limit):
    return pltpu.CompilerParams(vmem_limit_bytes=limit)


def record_span(positions, lengths_ref):
    start = jnp.zeros_like(positions)
    stop = jnp.full_like(positions, jnp.iinfo(jnp.int32).max)
    end = jnp.int32(0)
    for i in range(lengths_ref.shape[0]):
        end = end + lengths_ref[i]
        past = end <= positions
        start = jnp.where(past, end, start)
        stop = jnp.where(past, stop, jnp.minimum(stop, end))
    return start, stop


def device_index():
    return lax.axis_index("ctx") * lax.axis_size("head") + lax.axis_index("head")


def low_lanes(shape):
    return lax.broadcasted_iota(jnp.int32, shape, len(shape) - 1) % LANES < HD


def swap_halves(x):
    return pltpu.roll(x, HD, x.ndim - 1)


def zip_low(x, y):
    return jnp.where(low_lanes(x.shape), x, swap_halves(y))


def zip_high(x, y):
    return jnp.where(low_lanes(x.shape), swap_halves(x), y)


def conv_rows(padded_ref, cols, kernel_ref, lengths_ref, first_row, rows, flip):
    pos = first_row + lax.broadcasted_iota(jnp.int32, (rows, LANES), 0)
    start, stop = record_span(pos, lengths_ref)
    masks = []
    for t in range(KS):
        at = pos + (t - HALF)
        masks.append((at >= start) & (at < stop))
    pieces = []
    for c in cols:
        lanes = pl.ds(c * LANES, LANES)
        total = padded_ref[pl.ds(8, rows), lanes]
        for t in range(KS):
            tap = kernel_ref[KS - 1 - t if flip else t, lanes]
            shifted = padded_ref[pl.ds(8 - HALF + t, rows), lanes]
            total = total + jnp.where(masks[t], shifted, 0.0) * tap[None, :]
        pieces.append(total)
    return jnp.concatenate(pieces, axis=1)


def front_kernel(
    lengths_ref, before_ref, after_ref, x_hbm, taps_hbm, w_hbm, cot_hbm, wo_hbm,
    out_ref, x_ref, taps_ref, w_ref, cot_ref, wo_ref, padded, projected, d_rows, sems,
):
    rows, width = x_ref.shape
    blk = width // FRONT_STEPS

    def copy(source, target, i):
        return pltpu.make_async_copy(source, target, sems.at[i])

    whole = [
        copy(source, target, i)
        for i, (source, target) in enumerate(
            ((x_hbm, x_ref), (taps_hbm, taps_ref), (cot_hbm, cot_ref))
        )
    ]
    parts = []
    for step in range(FRONT_STEPS):
        part = pl.ds(step * blk, blk)
        at = 3 + 2 * step
        parts.append(
            (
                copy(w_hbm.at[part], w_ref.at[part], at),
                copy(wo_hbm.at[part], wo_ref.at[part], at + 1),
            )
        )
    for c in whole:
        c.start()
    for pair in parts:
        for c in pair:
            c.start()
    padded[pl.ds(0, 8), :] = before_ref[...].astype(F32)[EDGE - 8 :]
    padded[pl.ds(8 + rows, 8), :] = after_ref[...].astype(F32)[:8]
    for c in whole:
        c.wait()
    padded[pl.ds(8, rows), :] = x_ref[...].astype(F32)
    first_row = device_index() * rows
    per = blk // LANES
    for step in range(FRONT_STEPS):
        mixed = conv_rows(
            padded, range(step * per, (step + 1) * per), taps_ref, lengths_ref, first_row, rows,
            False,
        ).astype(BF16)
        parts[step][0].wait()
        part = jnp.dot(mixed, w_ref[pl.ds(step * blk, blk), :], preferred_element_type=F32)
        if step == 0:
            projected[...] = part
        else:
            projected[...] += part
        parts[step][1].wait()
        d_rows[:, pl.ds(step * blk, blk)] = lax.dot_general(
            cot_ref[...], wo_ref[pl.ds(step * blk, blk), :], (((1,), (1,)), ((), ())),
            preferred_element_type=F32,
        )
    for pair in range(width // LANES):
        lanes = pl.ds(pair * LANES, LANES)
        q, k, v = (projected[:, pl.ds(i * width + pair * LANES, LANES)] for i in range(3))
        d = d_rows[:, lanes]
        out_ref[2 * pair] = jnp.concatenate([zip_low(k, v), zip_low(q, d)]).astype(BF16)
        out_ref[2 * pair + 1] = jnp.concatenate([zip_high(k, v), zip_high(q, d)]).astype(BF16)


def front_call(lengths, before, x, after, taps, w_qkv, cotangent, w_out):
    rows, width = x.shape
    heads = width // HD
    smem = pl.BlockSpec(memory_space=pltpu.SMEM)
    vmem = pl.BlockSpec(memory_space=pltpu.VMEM)
    anywhere = pl.BlockSpec(memory_space=pl.ANY)
    return pl.pallas_call(
        front_kernel,
        in_specs=[smem, vmem, vmem] + [anywhere] * 5,
        out_specs=vmem,
        out_shape=jax.ShapeDtypeStruct((heads, 2 * rows, LANES), BF16),
        scratch_shapes=[
            pltpu.VMEM(x.shape, x.dtype),
            pltpu.VMEM(taps.shape, taps.dtype),
            pltpu.VMEM(w_qkv.shape, w_qkv.dtype),
            pltpu.VMEM(cotangent.shape, cotangent.dtype),
            pltpu.VMEM(w_out.shape, w_out.dtype),
            pltpu.VMEM((rows + 16, width), F32),
            pltpu.VMEM((rows, 3 * width), F32),
            pltpu.VMEM((rows, width), F32),
            pltpu.SemaphoreType.DMA((3 + 2 * FRONT_STEPS,)),
        ],
        compiler_params=params(VMEM_ALL),
        cost_estimate=pl.CostEstimate(
            flops=8 * rows * width * width, bytes_accessed=8 * width * width, transcendentals=0
        ),
        name="front",
    )(lengths, before, after, x, taps, w_qkv, cotangent, w_out)


def attention_kernel(
    pre, place, lengths_ref, kv_mine, kv_other, qd_ref,
    cq_ref, dkv_mine, edge_mine, send_ref,
    visit_q, visit_k, keys_ref, marked_ref, turned_ref, query_ref, qd_cat_ref, d_turned_ref, e_ref,
    total_ref, context_ref, row_ref, d_query_ref, acc_ref, cq_full,
):
    slots = qd_ref.shape[0]
    key_slots, rows, _ = kv_mine.shape
    tile = 2 * rows
    tiles, groups = key_slots // 2, slots // 2
    me = device_index()
    window = 2 * slots
    base, parity = me // window * (window * rows), me % 2
    origin = base - pre * tile
    unit = HD**-0.5
    to_exp2 = unit * math.log2(math.e)

    def row_at(slot, side):
        return slot * tile + side * rows + lax.broadcasted_iota(jnp.int32, (rows, 1), 0)

    lane = lax.broadcasted_iota(jnp.int32, (1, LANES), 1)
    starts = jnp.zeros((1, LANES), jnp.int32)
    stops = jnp.zeros((1, LANES), jnp.int32)
    end = jnp.int32(0)
    for i in range(lengths_ref.shape[0]):
        starts = jnp.where(lane == HD + i, end, starts)
        end = end + lengths_ref[i]
        stops = jnp.where(lane == HD + i, end, stops)

    count = jnp.int32(groups)
    for u in range(groups):
        visit_q[u] = u
        visit_k[u] = u + pre // 2
        first = base + u * (2 * tile) + parity * rows
        begin, end = jnp.int32(0), jnp.int32(0)
        for i in range(lengths_ref.shape[0]):
            end = end + lengths_ref[i]
            begin = jnp.where(end <= first, end, begin)
        t_first = jnp.maximum(begin - origin, 0) // (2 * tile)

        def note(t, count, u=u):
            visit_q[count] = u
            visit_k[count] = t
            return count + 1

        count = lax.fori_loop(t_first, u + pre // 2, note, count)
    for i in range(PER_STEP - 1):
        visit_q[count + i] = groups
        visit_k[count + i] = tiles

    low = low_lanes((rows, LANES))
    for t in range(tiles):
        for half, source in enumerate((kv_mine, kv_other)):
            side = parity if half == 0 else 1 - parity
            for i in range(2):
                block = source[place(2 * t + i, pre)]
                at = pl.ds(half * tile + i * rows, rows)
                keys_ref[t, at] = block
                turned_ref[t, :, at] = block.T
                pos = origin + row_at(2 * t + i, side)
                mark = jnp.where((pos >= starts) & (pos < stops), 0.0, FAR)
                marked_ref[t, at] = jnp.where(low, block.astype(F32), mark).astype(BF16)
    for ref in (keys_ref, marked_ref, turned_ref):
        ref[tiles] = jnp.zeros_like(ref[tiles])
    for ref in (query_ref, qd_cat_ref, row_ref):
        ref[groups] = jnp.zeros_like(ref[groups])
    for ref in (acc_ref, total_ref, context_ref, d_query_ref):
        ref[...] = jnp.zeros_like(ref)
    for u in range(groups):
        for i in range(2):
            qd = qd_ref[place(2 * u + i, 0), pl.ds(rows, rows)]
            at = pl.ds(i * rows, rows)
            d_turned_ref[u, :, at] = qd.T[HD:].astype(F32)
            qd = qd.astype(F32)
            pos = base + row_at(2 * u + i, parity)
            mark = jnp.where((pos >= starts) & (pos < stops), 1.0, 0.0)
            query_ref[u, at] = jnp.where(low, qd, mark).astype(BF16)
            qd_cat_ref[u, at] = jnp.where(low, qd, 0.0).astype(BF16)
            qd_cat_ref[u, pl.ds(tile + i * rows, rows)] = jnp.where(low, 0.0, qd).astype(BF16)

    nt = (((1,), (1,)), ((), ()))
    chunks = [pl.ds(c * rows, rows) for c in range(4)]
    q_lane = lax.broadcasted_iota(jnp.int32, (rows, tile), 1)
    q_row = q_lane // rows * tile + q_lane % rows + parity * rows
    k_sub = lax.broadcasted_iota(jnp.int32, (rows, tile), 0)

    def forward(i, diagonal):
        u, t = visit_q[i], visit_k[i]
        total = jnp.zeros((8, tile), F32)
        halves = []
        for c, at in enumerate(chunks):
            scores = lax.dot_general(
                marked_ref[t, at], query_ref[u], nt, preferred_element_type=F32
            )
            e = jnp.exp2(scores * to_exp2)
            if diagonal:
                side = parity if c < 2 else 1 - parity
                e = jnp.where(k_sub + (c % 2 * tile + side * rows) <= q_row, e, 0.0)
            e_ref[i, at] = e
            total = total + jnp.sum(e.reshape(rows // 8, 8, tile), axis=0)
            halves.append(e.astype(BF16))
        context = jnp.dot(
            turned_ref[t, HD:], jnp.concatenate(halves), preferred_element_type=F32
        )
        return u, total, context

    def forward_some(diagonal):
        def run(j, carry):
            for u, total, context in [
                forward(PER_STEP * j + i, diagonal) for i in range(PER_STEP)
            ]:
                total_ref[u] += total
                context_ref[u] += context
            return carry

        return run

    steps = (count + PER_STEP - 1) // PER_STEP
    lax.fori_loop(0, groups // PER_STEP, forward_some(True), 0)
    lax.fori_loop(groups // PER_STEP, steps, forward_some(False), 0)
    for u in range(groups):
        inverse = 1.0 / jnp.sum(total_ref[u], axis=0, keepdims=True)
        context = (context_ref[u] * inverse).astype(BF16).astype(F32)
        context_ref[u] = context
        row_ref[u, pl.ds(0, 1)] = inverse
        row_ref[u, pl.ds(1, 1)] = jnp.sum(d_turned_ref[u] * context, axis=0, keepdims=True)

    def backward(i):
        u, t = visit_q[i], visit_k[i]
        row = row_ref[u]
        halves, d_keys = [], []
        for at in chunks:
            probs = e_ref[i, at] * row[0:1]
            d_probs = lax.dot_general(
                keys_ref[t, at], qd_cat_ref[u, pl.ds(tile, tile)], nt, preferred_element_type=F32
            )
            d_scores = (probs * (d_probs - row[1:2])).astype(BF16)
            both = jnp.concatenate([d_scores, probs.astype(BF16)], axis=1)
            d_keys.append(jnp.dot(both, qd_cat_ref[u], preferred_element_type=F32))
            halves.append(d_scores)
        d_queries = jnp.dot(
            turned_ref[t, :HD], jnp.concatenate(halves), preferred_element_type=F32
        )
        return u, t, d_keys, d_queries

    def backward_some(j, carry):
        for u, t, d_keys, d_queries in [backward(PER_STEP * j + i) for i in range(PER_STEP)]:
            for at, part in zip(chunks, d_keys):
                acc_ref[t, at] += part
            d_query_ref[u] += d_queries
        return carry

    lax.fori_loop(0, steps, backward_some, 0)
    for u in range(groups):
        packed = jnp.concatenate([context_ref[u], d_query_ref[u] * unit], axis=0).T
        for i in range(2):
            part = packed[i * rows : (i + 1) * rows]
            cq_full[2 * u + i] = part
            cq_ref[2 * u + i] = part.astype(BF16)
    scale = jnp.where(low_lanes((1, LANES)), unit, 1.0)
    head = lax.broadcasted_iota(jnp.int32, (8, LANES), 0) < 4

    def end_rows(half, slot, first):
        slot = pre + jnp.clip(slot, 0, slots - 1)
        at = half * tile + slot % 2 * rows + first
        return acc_ref[slot // 2, pl.ds(pl.multiple_of(at, 8), 8)] * scale

    for s in range(key_slots):
        part = pl.ds(s % 2 * rows, rows)
        dkv_mine[s] = acc_ref[s // 2, part] * scale
        part = pl.ds(tile + s % 2 * rows, rows)
        send_ref[s, pl.ds(0, rows)] = (acc_ref[s // 2, part] * scale).astype(BF16)
        if s < pre:
            send_ref[s, pl.ds(rows, 16)] = jnp.zeros((16, LANES), BF16)
    for s in range(slots):
        edge_mine[s] = jnp.where(
            head, end_rows(1, s + parity, 0), end_rows(1, s - 1 + parity, rows - 8)
        )
        past, later = s - parity, s + 1 - parity
        d_edge = jnp.where(head, end_rows(0, later, 0), end_rows(0, past, rows - 8))
        q_edge = jnp.where(
            head,
            cq_full[jnp.clip(later, 0, slots - 1), pl.ds(0, 8)],
            cq_full[jnp.clip(past, 0, slots - 1), pl.ds(rows - 8, 8)],
        )
        send_ref[pre + s, pl.ds(rows, 16)] = jnp.concatenate([d_edge, q_edge]).astype(BF16)


def attention_call(lengths, kv_mine, kv_other, qd, pre):
    slots = qd.shape[0]
    key_slots, rows, _ = kv_mine.shape
    tile = 2 * rows
    tiles, groups = key_slots // 2, slots // 2
    reach = MAXLEN // (2 * tile) + 1
    place = lambda s, ordered: s if ordered else bit_reversed(s, slots)
    visits = sum(min(u + pre // 2 + 1, reach) for u in range(groups)) + PER_STEP - 1
    smem = pl.BlockSpec(memory_space=pltpu.SMEM)
    vmem = pl.BlockSpec(memory_space=pltpu.VMEM)
    return pl.pallas_call(
        functools.partial(attention_kernel, pre, place),
        in_specs=[smem, vmem, vmem, vmem],
        out_specs=[vmem, vmem, vmem, vmem],
        out_shape=[
            jax.ShapeDtypeStruct((slots, rows, LANES), BF16),
            jax.ShapeDtypeStruct((key_slots, rows, LANES), F32),
            jax.ShapeDtypeStruct((slots, 8, LANES), F32),
            jax.ShapeDtypeStruct((key_slots, rows + 16, LANES), BF16),
        ],
        scratch_shapes=[
            pltpu.SMEM((visits,), jnp.int32),
            pltpu.SMEM((visits,), jnp.int32),
            pltpu.VMEM((tiles + 1, 2 * tile, LANES), BF16),
            pltpu.VMEM((tiles + 1, 2 * tile, LANES), BF16),
            pltpu.VMEM((tiles + 1, LANES, 2 * tile), BF16),
            pltpu.VMEM((groups + 1, tile, LANES), BF16),
            pltpu.VMEM((groups + 1, 2 * tile, LANES), BF16),
            pltpu.VMEM((groups, HD, tile), F32),
            pltpu.VMEM((visits, 2 * tile, tile), F32),
            pltpu.VMEM((groups + 1, 8, tile), F32),
            pltpu.VMEM((groups + 1, HD, tile), F32),
            pltpu.VMEM((groups + 1, 8, tile), F32),
            pltpu.VMEM((groups + 1, HD, tile), F32),
            pltpu.VMEM((tiles + 1, 2 * tile, LANES), F32),
            pltpu.VMEM((slots, rows, LANES), F32),
        ],
        compiler_params=params(VMEM_MOST),
        cost_estimate=pl.CostEstimate(
            flops=10 * slots * rows * MAXLEN * LANES,
            bytes_accessed=20 * slots * rows * LANES,
            transcendentals=slots * rows * MAXLEN,
        ),
        name="attention",
    )(lengths, kv_mine, kv_other, qd)


def combine_kernel(cq_ref, mine_ref, edge_ref, got_ref, out_ref):
    slots, rows, _ = cq_ref.shape
    for s in range(slots):
        at = bit_reversed(s, slots)
        out_ref[at, pl.ds(0, rows)] = cq_ref[s]
        got = got_ref[s].astype(F32)
        out_ref[at, pl.ds(rows, rows)] = (mine_ref[s] + got[:rows]).astype(BF16)
        edges = [edge_ref[s] + got[rows : rows + 8], got[rows + 8 :]]
        out_ref[at, pl.ds(2 * rows, 16)] = jnp.concatenate(edges).astype(BF16)


def combine_call(cq, mine, edge, got):
    slots, rows, _ = cq.shape
    vmem = pl.BlockSpec(memory_space=pltpu.VMEM)
    return pl.pallas_call(
        combine_kernel,
        in_specs=[vmem] * 4,
        out_specs=vmem,
        out_shape=jax.ShapeDtypeStruct((slots, 2 * rows + 16, LANES), BF16),
        compiler_params=params(VMEM_SOME),
        name="combine",
    )(cq, mine, edge, got)


def combine_windows(cq, mine, got, pre, side, window, devices):
    slots, rows, _ = cq.shape
    dkv = mine + got[:, :rows].astype(F32)
    back = [(i + window, i) for i in range(devices - window)]
    earlier = lax.ppermute(dkv[:pre].astype(BF16), AXES, back).astype(F32)
    dkv = dkv[pre:].at[slots - pre :].add(earlier).astype(BF16)
    both = jnp.concatenate([cq, dkv], axis=2)
    tails, heads = both[:, rows - 8 :], both[:, :8]
    swapped = [(i, i ^ 1) for i in range(devices)]
    tails_other = lax.ppermute(tails, AXES, swapped)
    heads_other = lax.ppermute(heads, AXES, swapped)
    last = [(i, i + window - 1) for i in range(1, devices - window, 2)]
    tail_past = lax.ppermute(tails[-1:], AXES, last)
    head_next = lax.ppermute(heads[:1], AXES, [(j, i) for i, j in last])
    before = jnp.where(
        side == 0, jnp.concatenate([tail_past, tails_other[:-1]]), tails_other
    )
    after = jnp.where(side == 0, heads_other, jnp.concatenate([heads_other[1:], head_next]))
    edge = jnp.where(jnp.arange(8)[None, :, None] < 4, after, before)
    grads = jnp.concatenate([cq, dkv, edge[..., LANES:], edge[..., :LANES]], axis=1)
    return jnp.stack([grads[bit_reversed(s, slots)] for s in range(slots)])


def back_kernel(
    lengths_ref, r_ref, taps_ref, w_ref, wo_ref, attended_ref, grad_ref, context, grads, padded
):
    heads = r_ref.shape[0]
    rows, width = context.shape
    blk = width // BACK_STEPS
    main, dkv = slice(0, rows), slice(rows, 2 * rows)
    edge_dkv, edge_cq = slice(2 * rows, 2 * rows + 8), slice(2 * rows + 8, 2 * rows + 16)
    pad = jnp.zeros((8, LANES), F32)
    for pair in range(heads // 2):
        lanes = pl.ds(pair * LANES, LANES)
        x, y = (r_ref[2 * pair + i].astype(F32) for i in range(2))
        context[:, lanes] = zip_low(x[main], y[main]).astype(BF16)

        def gather(mix, part, edge):
            return jnp.concatenate([mix(x[part], y[part]), mix(x[edge], y[edge]), pad]).astype(BF16)

        grads[:, lanes] = gather(zip_high, main, edge_cq)
        grads[:, pl.ds(width + pair * LANES, LANES)] = gather(zip_low, dkv, edge_dkv)
        grads[:, pl.ds(2 * width + pair * LANES, LANES)] = gather(zip_high, dkv, edge_dkv)
    first_row = device_index() * rows
    per = blk // LANES
    for step in range(BACK_STEPS):
        part = pl.ds(step * blk, blk)
        mixed = lax.dot_general(
            grads[...], w_ref[part, :], (((1,), (1,)), ((), ())), preferred_element_type=F32
        ).astype(BF16).astype(F32)
        edge = mixed[rows : rows + 8]
        padded[pl.ds(0, 8), part] = edge
        padded[pl.ds(8, rows), part] = mixed[:rows]
        padded[pl.ds(8 + rows, 8), part] = edge
        attended_ref[:, part] = jnp.dot(
            context[...], wo_ref[:, part], preferred_element_type=F32
        ).astype(BF16)
        grad_ref[:, part] = conv_rows(
            padded, range(step * per, (step + 1) * per), taps_ref, lengths_ref, first_row, rows,
            True,
        ).astype(BF16)


def back_call(lengths, r, taps, w_qkv, w_out):
    heads = r.shape[0]
    rows = (r.shape[1] - 16) // 2
    width = heads * HD
    smem = pl.BlockSpec(memory_space=pltpu.SMEM)
    vmem = pl.BlockSpec(memory_space=pltpu.VMEM)
    shape = jax.ShapeDtypeStruct((rows, width), BF16)
    return pl.pallas_call(
        back_kernel,
        in_specs=[smem, vmem, vmem, vmem, vmem],
        out_specs=[vmem, vmem],
        out_shape=[shape, shape],
        scratch_shapes=[
            pltpu.VMEM((rows, width), BF16),
            pltpu.VMEM((rows + 16, 3 * width), BF16),
            pltpu.VMEM((rows + 16, width), F32),
        ],
        compiler_params=params(VMEM_SOME),
        cost_estimate=pl.CostEstimate(
            flops=8 * rows * width * width, bytes_accessed=8 * width * width, transcendentals=0
        ),
        name="back",
    )(lengths, r, taps, w_qkv, w_out)


def bit_reversed(i, count):
    bits = count.bit_length() - 1
    if count != 1 << bits:
        return i
    return sum((i >> b & 1) << (bits - 1 - b) for b in range(bits))


def on_device(tokens, conv_kernel, w_qkv, w_out, lengths, cotangent):
    rows, width = tokens.shape
    heads = width // HD
    devices = lax.axis_size(AXES)
    window = 2 * heads
    windows = devices // window
    pre = MAXLEN // (2 * rows) if windows > 1 else 0
    me = lax.axis_index(AXES)
    same_side = [
        [w * window + 2 * bit_reversed(c, heads) + side for c in range(heads)]
        for w in range(windows)
        for side in range(2)
    ]
    swapped = [(i, i ^ 1) for i in range(devices)]
    up = [(i, i + 1) for i in range(devices - 1)]
    down = [(i + 1, i) for i in range(devices - 1)]

    def exchange(x):
        return lax.all_to_all(
            x, AXES, split_axis=0, concat_axis=0, axis_index_groups=same_side, tiled=True
        )

    before = lax.ppermute(tokens[rows - EDGE :], AXES, up)
    after = lax.ppermute(tokens[:EDGE], AXES, down)
    sent = front_call(lengths, before, tokens, after, conv_kernel, w_qkv, cotangent, w_out)
    qd = exchange(sent)
    kv_mine = qd[:, :rows]
    if pre:
        shift = [(i, i + window) for i in range(devices - window)]
        kv_mine = jnp.stack([kv_mine[bit_reversed(s, heads)] for s in range(heads)])
        kv_mine = jnp.concatenate([lax.ppermute(kv_mine[heads - pre :], AXES, shift), kv_mine])
    kv_other = lax.ppermute(kv_mine, AXES, swapped)
    cq, mine, edge, send = attention_call(lengths, kv_mine, kv_other, qd, pre)
    got = lax.ppermute(send, AXES, swapped)
    if pre:
        grads = combine_windows(cq, mine, got, pre, me % 2, window, devices)
    else:
        grads = combine_call(cq, mine, edge, got)
    return back_call(lengths, exchange(grads), conv_kernel, w_qkv, w_out)


def solution(mesh):
    placed = (P(AXES, None), P(), P(), P(), P(), P(AXES, None))
    return jax.shard_map(
        on_device,
        mesh=mesh,
        in_specs=placed,
        out_specs=(P(AXES, None), P(AXES, None)),
        check_vma=False,
    )
```

profile of v0, /device:TPU:0, one launch (start us, length us, event | category | flops | bytes accessed | tf_op | source)
XLA Modules:
  0.0 117.3 jit_solution(4203999528383771379)
XLA Ops:
  0.6 0.8 fusion
  1.4 1.3 %collective-permute-start.1 = (bf16[16,1024]{1,0:T(8,128)(2,1)S(1)}, bf16[16,1024]{1,0:T(8,128)(2,1)S(1)}, u32[]{:S(2)}, u32[]{:S(2)}) collective-permute-start(bf16[16,1024]{1,0:T(8,128)(2,1)S(1)} %get-tuple-element.10), channel_id=1, source_target_pairs={{1,0},{2,1},{3,2},{4,3},{5,4},{6,5},{7,6},{8,7},{9,8},{10,9},{11,1... | collective-permute-start | bytes 98312 | tf_op jit(solution)/shard_map/ppermute | solution.py:553
  2.7 3.0 %collective-permute-start = (bf16[16,1024]{1,0:T(8,128)(2,1)S(1)}, bf16[16,1024]{1,0:T(8,128)(2,1)S(1)}, u32[]{:S(2)}, u32[]{:S(2)}) collective-permute-start(bf16[16,1024]{1,0:T(8,128)(2,1)S(1)} %get-tuple-element.11), channel_id=1, source_target_pairs={{0,1},{1,2},{2,3},{3,4},{4,5},{5,6},{6,7},{7,8},{8,9},{9,10},{10,1... | collective-permute-start | bytes 98312 | tf_op jit(solution)/shard_map/ppermute | solution.py:552
  5.7 0.0 collective-permute-done.1.after_ref
  5.7 0.0 copy-start.3
  5.8 0.8 collective-permute-done.before_ref
  6.6 0.0 copy-done.3
  6.6 0.6 copy-done.4
  7.2 7.7 %front.1 = bf16[16,256,128]{2,1,0:T(8,128)(2,1)} custom-call(s32[4]{0:T(128)} %lengths_ref.5, bf16[16,1024]{1,0:T(8,128)(2,1)} %copy-done.4, bf16[16,1024]{1,0:T(8,128)(2,1)} %copy-done.3, bf16[128,1024]{1,0:T(8,128)(2,1)} %x_hbm.1, f32[7,1024]{1,0:T(8,128)} %taps_ref.1, bf16[1024,3072]{1,0:T(8,128)(2,1)} %w_ref.1, bf16[128,1024]{1,0:T(8,128)(2,1)} %cot_hbm.1, ...), custom_call_target="tpu_custom_call" | custom-call | flops 1073741824 | bytes 8388608 | tf_op jit(solution)/shard_map/front/pallas_call | solution.py:152
  14.9 0.0 copy-start.2
  14.9 36.3 %all_to_all.10.qd_ref = bf16[16,256,128]{2,1,0:T(8,128)(2,1)S(1)} all-to-all(bf16[16,256,128]{2,1,0:T(8,128)(2,1)} %front.1), channel_id=1, replica_groups={{0,16,8,24,4,20,12,28,2,18,10,26,6,22,14,30},{1,17,9,25,5,21,13,29,3,19..., dimensions={0} | all-to-all | bytes 2097152 | tf_op jit(solution)/shard_map/all_to_all | solution.py:548
  51.3 0.0 slice-start.1
  51.3 0.1 collective-permute-start.2
  51.4 1.9 %collective-permute-done.2.kv_other = bf16[16,128,128]{2,1,0:T(8,128)(2,1)S(1)} collective-permute-done((bf16[16,128,128]{2,1,0:T(8,128)(2,1)S(1)}, bf16[16,128,128]{2,1,0:T(8,128)(2,1)S(1)}, u32[]{:S(2)}, u32[]{:S(2)}) %collective-permute-start.2) | collective-permute-done | bytes 524320 | tf_op jit(solution)/shard_map/ppermute | solution.py:561
  53.3 0.0 copy-done.2
  53.3 24.1 %attention.1 = (bf16[16,128,128]{2,1,0:T(8,128)(2,1)S(1)}, f32[16,128,128]{2,1,0:T(8,128)S(1)}, f32[16,8,128]{2,1,0:T(8,128)S(1)}, bf16[16,144,128]{2,1,0:T(8,128)(2,1)S(1)}) custom-call(s32[4]{0:T(128)S(1)} %copy-done.2, bf16[16,128,128]{2,1,0:T(8,128)(2,1)S(1)} %slice.12.kv_mine, bf16[16,128,128]{2,1,0:T(8,128)(2,1)S(1)} %collective-permute-done.2.kv_other, ...), custom_call_target="tpu_custom_call" | custom-call | flops 5368709120 | bytes 5242880 | tf_op jit(solution)/shard_map/attention/pallas_call | solution.py:374
  77.4 0.2 collective-permute-start.3
  77.6 1.9 %collective-permute-done.3.got_ref = bf16[16,144,128]{2,1,0:T(8,128)(2,1)S(1)} collective-permute-done((bf16[16,144,128]{2,1,0:T(8,128)(2,1)S(1)}, bf16[16,144,128]{2,1,0:T(8,128)(2,1)S(1)}, u32[]{:S(2)}, u32[]{:S(2)}) %collective-permute-start.3) | collective-permute-done | bytes 589856 | tf_op jit(solution)/shard_map/ppermute | solution.py:563
  79.4 0.2 combine.1
  79.6 32.9 %all_to_all.11.r_ref = bf16[16,272,128]{2,1,0:T(8,128)(2,1)S(1)} all-to-all(bf16[16,272,128]{2,1,0:T(8,128)(2,1)S(1)} %combine.1), channel_id=1, replica_groups={{0,16,8,24,4,20,12,28,2,18,10,26,6,22,14,30},{1,17,9,25,5,21,13,29,3,19..., dimensions={0} | all-to-all | bytes 2228224 | tf_op jit(solution)/shard_map/all_to_all | solution.py:548
  112.5 0.0 slice-done
  112.5 0.0 slice-done.1
  112.5 0.0 copy-done
  112.5 4.8 %back.1 = (bf16[128,1024]{1,0:T(8,128)(2,1)}, bf16[128,1024]{1,0:T(8,128)(2,1)}) custom-call(s32[4]{0:T(128)S(1)} %copy-done.2, bf16[16,272,128]{2,1,0:T(8,128)(2,1)S(1)} %all_to_all.11.r_ref, f32[7,1024]{1,0:T(8,128)S(1)} %copy-done.1, bf16[1024,3072]{1,0:T(8,128)(2,1)S(1)} %bitcast.1, bf16[1024,1024]{1,0:T(8,128)(2,1)S(1)} %copy-done), custom_call_target="tpu_custom_call" | custom-call | flops 1073741824 | bytes 8388608 | tf_op jit(solution)/shard_map/back/pallas_call | solution.py:505
  (7 shorter events, 0.0 us)
Async XLA Ops:
  1.4 4.3 %collective-permute-start.1 = (bf16[16,1024]{1,0:T(8,128)(2,1)S(1)}, bf16[16,1024]{1,0:T(8,128)(2,1)S(1)}, u32[]{:S(2)}, u32[]{:S(2)}) collective-permute-start(bf16[16,1024]{1,0:T(8,128)(2,1)S(1)} %get-tuple-element.10), channel_id=1, source_target_pairs={{1,0},{2,1},{3,2},{4,3},{5,4},{6,5},{7,6},{8,7},{9,8},{10,9},{11,1... | collective-permute-start | bytes 98312 | tf_op jit(solution)/shard_map/ppermute | solution.py:553
  2.7 3.9 %collective-permute-start = (bf16[16,1024]{1,0:T(8,128)(2,1)S(1)}, bf16[16,1024]{1,0:T(8,128)(2,1)S(1)}, u32[]{:S(2)}, u32[]{:S(2)}) collective-permute-start(bf16[16,1024]{1,0:T(8,128)(2,1)S(1)} %get-tuple-element.11), channel_id=1, source_target_pairs={{0,1},{1,2},{2,3},{3,4},{4,5},{5,6},{6,7},{7,8},{8,9},{9,10},{10,1... | collective-permute-start | bytes 98312 | tf_op jit(solution)/shard_map/ppermute | solution.py:552
  5.7 0.8 copy-start.3
  6.6 0.6 copy-start.4
  14.9 38.4 %copy-start.2 = (s32[4]{0:T(128)S(1)}, s32[4]{0:T(128)}, u32[]{:S(2)}) copy-start(s32[4]{0:T(128)} %lengths_ref.5) | copy-start | bytes 52
  51.2 61.3 %slice-start = ((s8[6291456]{0:T(1024)(128)(4,1)}), s8[4194304]{0:T(1024)(128)(4,1)S(1)}, s32[]{:S(2)}) async-start(s8[6291456]{0:T(1024)(128)(4,1)} %bitcast), calls=%async_computation.2 | async-start | bytes 8388608
  51.3 61.2 %slice-start.1 = ((s8[6291456]{0:T(1024)(128)(4,1)}), s8[2097152]{0:T(1024)(128)(4,1)S(1)}, s32[]{:S(2)}) async-start(s8[6291456]{0:T(1024)(128)(4,1)} %bitcast), calls=%async_computation.3 | async-start | bytes 4194304
  51.3 2.0 %collective-permute-start.2 = (bf16[16,128,128]{2,1,0:T(8,128)(2,1)S(1)}, bf16[16,128,128]{2,1,0:T(8,128)(2,1)S(1)}, u32[]{:S(2)}, u32[]{:S(2)}) collective-permute-start(bf16[16,128,128]{2,1,0:T(8,128)(2,1)S(1)} %slice.12.kv_mine), channel_id=1, source_target_pairs={{0,1},{1,0},{2,3},{3,2},{4,5},{5,4},{6,7},{7,6},{8,9},{9,8},{10,11... | collective-permute-start | bytes 1572872 | tf_op jit(solution)/shard_map/ppermute | solution.py:561
  77.4 2.1 %collective-permute-start.3 = (bf16[16,144,128]{2,1,0:T(8,128)(2,1)S(1)}, bf16[16,144,128]{2,1,0:T(8,128)(2,1)S(1)}, u32[]{:S(2)}, u32[]{:S(2)}) collective-permute-start(bf16[16,144,128]{2,1,0:T(8,128)(2,1)S(1)} %get-tuple-element.9), channel_id=1, source_target_pairs={{0,1},{1,0},{2,3},{3,2},{4,5},{5,4},{6,7},{7,6},{8,9},{9,8},{10,11... | collective-permute-start | bytes 1769480 | tf_op jit(solution)/shard_map/ppermute | solution.py:563
  79.4 33.1 %copy-start = (bf16[1024,1024]{1,0:T(8,128)(2,1)S(1)}, bf16[1024,1024]{1,0:T(8,128)(2,1)}, u32[]{:S(2)}) copy-start(bf16[1024,1024]{1,0:T(8,128)(2,1)} %wo_ref.1) | copy-start | bytes 6291460
  79.4 33.1 %copy-start.1 = (f32[7,1024]{1,0:T(8,128)S(1)}, f32[7,1024]{1,0:T(8,128)}, u32[]{:S(2)}) copy-start(f32[7,1024]{1,0:T(8,128)} %taps_ref.1) | copy-start | bytes 86020
where the time goes:
time: 118 us; the launch traced here: 117 us
  blocking collectives  69.2 us (59%)
  Pallas kernels  36.7 us (31%)
  starting transfers between devices  4.59 us (4%)
  waiting for transfers between devices  4.58 us (4%)
  local copies, waits for them, and re-layouts  1.47 us (1%)
    all_to_all x2, blocking collectives, exchange(): lax.all_to_all(x, AXES, split_axis=0, concat_axis=0, axis_index_groups=sa...  69.2 us
    pallas_call x1, Pallas kernels, attention_call(): pl.pallas_call(functools.partial(attention_kernel, pre, place), in_specs=...  24.1 us
    pallas_call x1, Pallas kernels, front_call(): pl.pallas_call(front_kernel, in_specs=[smem, vmem, vmem] + [anywhere] * 5...  7.66 us
    pallas_call x1, Pallas kernels, back_call(): pl.pallas_call(back_kernel, in_specs=[smem, vmem, vmem, vmem, vmem], out_...  4.76 us
    ppermute x1, starting transfers between devices, on_device(): before = lax.ppermute(tokens[rows - EDGE:], AXES, up)  3.03 us
  transfers between devices with their start and end apart: 4, of which 3 were waited for; matrix products, arithmetic and copies ran while one was open for 0% of the time, Pallas kernels for 0%

commit v1 on v0

--- a/solution.py
+++ b/solution.py
@@ -15,7 +15,7 @@
 AXES = ("ctx", "head")
 LANES = 128
 EDGE = 16
-PER_STEP = 2
+PER_STEP = 4
 FAR = -1e30
 FRONT_STEPS = 4
 BACK_STEPS = 4
@@ -219,9 +219,6 @@
             return count + 1
 
         count = lax.fori_loop(t_first, u + pre // 2, note, count)
-    for i in range(PER_STEP - 1):
-        visit_q[count + i] = groups
-        visit_k[count + i] = tiles
 
     low = low_lanes((rows, LANES))
     for t in range(tiles):
@@ -235,10 +232,6 @@
                 pos = origin + row_at(2 * t + i, side)
                 mark = jnp.where((pos >= starts) & (pos < stops), 0.0, FAR)
                 marked_ref[t, at] = jnp.where(low, block.astype(F32), mark).astype(BF16)
-    for ref in (keys_ref, marked_ref, turned_ref):
-        ref[tiles] = jnp.zeros_like(ref[tiles])
-    for ref in (query_ref, qd_cat_ref, row_ref):
-        ref[groups] = jnp.zeros_like(ref[groups])
     for ref in (acc_ref, total_ref, context_ref, d_query_ref):
         ref[...] = jnp.zeros_like(ref)
     for u in range(groups):
@@ -254,35 +247,27 @@
             qd_cat_ref[u, pl.ds(tile + i * rows, rows)] = jnp.where(low, 0.0, qd).astype(BF16)
 
     nt = (((1,), (1,)), ((), ()))
-    chunks = [pl.ds(c * rows, rows) for c in range(4)]
-    q_lane = lax.broadcasted_iota(jnp.int32, (rows, tile), 1)
+    wide = (2 * tile, tile)
+    q_lane = lax.broadcasted_iota(jnp.int32, wide, 1)
     q_row = q_lane // rows * tile + q_lane % rows + parity * rows
-    k_sub = lax.broadcasted_iota(jnp.int32, (rows, tile), 0)
+    k_sub = lax.broadcasted_iota(jnp.int32, wide, 0)
+    side = jnp.where(k_sub < tile, parity, 1 - parity)
+    causal = k_sub // rows % 2 * tile + k_sub % rows + side * rows <= q_row
 
     def forward(i, diagonal):
         u, t = visit_q[i], visit_k[i]
-        total = jnp.zeros((8, tile), F32)
-        halves = []
-        for c, at in enumerate(chunks):
-            scores = lax.dot_general(
-                marked_ref[t, at], query_ref[u], nt, preferred_element_type=F32
-            )
-            e = jnp.exp2(scores * to_exp2)
-            if diagonal:
-                side = parity if c < 2 else 1 - parity
-                e = jnp.where(k_sub + (c % 2 * tile + side * rows) <= q_row, e, 0.0)
-            e_ref[i, at] = e
-            total = total + jnp.sum(e.reshape(rows // 8, 8, tile), axis=0)
-            halves.append(e.astype(BF16))
-        context = jnp.dot(
-            turned_ref[t, HD:], jnp.concatenate(halves), preferred_element_type=F32
-        )
-        return u, total, context
-
-    def forward_some(diagonal):
+        scores = lax.dot_general(marked_ref[t], query_ref[u], nt, preferred_element_type=F32)
+        e = jnp.exp2(scores * to_exp2)
+        if diagonal:
+            e = jnp.where(causal, e, 0.0)
+        e_ref[i] = e
+        context = jnp.dot(turned_ref[t, HD:], e.astype(BF16), preferred_element_type=F32)
+        return u, jnp.sum(e.reshape(2 * tile // 8, 8, tile), axis=0), context
+
+    def forward_some(diagonal, first, per):
         def run(j, carry):
             for u, total, context in [
-                forward(PER_STEP * j + i, diagonal) for i in range(PER_STEP)
+                forward(first + per * j + i, diagonal) for i in range(per)
             ]:
                 total_ref[u] += total
                 context_ref[u] += context
@@ -290,9 +275,14 @@
 
         return run
 
-    steps = (count + PER_STEP - 1) // PER_STEP
-    lax.fori_loop(0, groups // PER_STEP, forward_some(True), 0)
-    lax.fori_loop(groups // PER_STEP, steps, forward_some(False), 0)
+    def run_all(make, first, last):
+        steps = (last - first) // PER_STEP
+        lax.fori_loop(0, steps, make(first, PER_STEP), 0)
+        rest = first + steps * PER_STEP
+        lax.fori_loop(0, last - rest, make(rest, 1), 0)
+
+    lax.fori_loop(0, groups // PER_STEP, forward_some(True, 0, PER_STEP), 0)
+    run_all(functools.partial(forward_some, False), groups, count)
     for u in range(groups):
         inverse = 1.0 / jnp.sum(total_ref[u], axis=0, keepdims=True)
         context = (context_ref[u] * inverse).astype(BF16).astype(F32)
@@ -303,29 +293,28 @@
     def backward(i):
         u, t = visit_q[i], visit_k[i]
         row = row_ref[u]
-        halves, d_keys = [], []
-        for at in chunks:
-            probs = e_ref[i, at] * row[0:1]
-            d_probs = lax.dot_general(
-                keys_ref[t, at], qd_cat_ref[u, pl.ds(tile, tile)], nt, preferred_element_type=F32
-            )
-            d_scores = (probs * (d_probs - row[1:2])).astype(BF16)
-            both = jnp.concatenate([d_scores, probs.astype(BF16)], axis=1)
-            d_keys.append(jnp.dot(both, qd_cat_ref[u], preferred_element_type=F32))
-            halves.append(d_scores)
-        d_queries = jnp.dot(
-            turned_ref[t, :HD], jnp.concatenate(halves), preferred_element_type=F32
-        )
+        probs = e_ref[i] * row[0:1]
+        d_probs = lax.dot_general(
+            keys_ref[t], qd_cat_ref[u, pl.ds(tile, tile)], nt, preferred_element_type=F32
+        )
+        d_scores = (probs * (d_probs - row[1:2])).astype(BF16)
+        both = jnp.concatenate([d_scores, probs.astype(BF16)], axis=1)
+        d_keys = jnp.dot(both, qd_cat_ref[u], preferred_element_type=F32)
+        d_queries = jnp.dot(turned_ref[t, :HD], d_scores, preferred_element_type=F32)
         return u, t, d_keys, d_queries
 
-    def backward_some(j, carry):
-        for u, t, d_keys, d_queries in [backward(PER_STEP * j + i) for i in range(PER_STEP)]:
-            for at, part in zip(chunks, d_keys):
-                acc_ref[t, at] += part
-            d_query_ref[u] += d_queries
-        return carry
-
-    lax.fori_loop(0, steps, backward_some, 0)
+    def backward_some(first, per):
+        def run(j, carry):
+            for u, t, d_keys, d_queries in [
+                backward(first + per * j + i) for i in range(per)
+            ]:
+                acc_ref[t] += d_keys
+                d_query_ref[u] += d_queries
+            return carry
+
+        return run
+
+    run_all(backward_some, 0, count)
     for u in range(groups):
         packed = jnp.concatenate([context_ref[u], d_query_ref[u] * unit], axis=0).T
         for i in range(2):
@@ -368,7 +357,7 @@
     tiles, groups = key_slots // 2, slots // 2
     reach = MAXLEN // (2 * tile) + 1
     place = lambda s, ordered: s if ordered else bit_reversed(s, slots)
-    visits = sum(min(u + pre // 2 + 1, reach) for u in range(groups)) + PER_STEP - 1
+    visits = sum(min(u + pre // 2 + 1, reach) for u in range(groups))
     smem = pl.BlockSpec(memory_space=pltpu.SMEM)
     vmem = pl.BlockSpec(memory_space=pltpu.VMEM)
     return pl.pallas_call(
@@ -384,18 +373,18 @@
         scratch_shapes=[
             pltpu.SMEM((visits,), jnp.int32),
             pltpu.SMEM((visits,), jnp.int32),
-            pltpu.VMEM((tiles + 1, 2 * tile, LANES), BF16),
-            pltpu.VMEM((tiles + 1, 2 * tile, LANES), BF16),
-            pltpu.VMEM((tiles + 1, LANES, 2 * tile), BF16),
-            pltpu.VMEM((groups + 1, tile, LANES), BF16),
-            pltpu.VMEM((groups + 1, 2 * tile, LANES), BF16),
+            pltpu.VMEM((tiles, 2 * tile, LANES), BF16),
+            pltpu.VMEM((tiles, 2 * tile, LANES), BF16),
+            pltpu.VMEM((tiles, LANES, 2 * tile), BF16),
+            pltpu.VMEM((groups, tile, LANES), BF16),
+            pltpu.VMEM((groups, 2 * tile, LANES), BF16),
             pltpu.VMEM((groups, HD, tile), F32),
             pltpu.VMEM((visits, 2 * tile, tile), F32),
-            pltpu.VMEM((groups + 1, 8, tile), F32),
-            pltpu.VMEM((groups + 1, HD, tile), F32),
-            pltpu.VMEM((groups + 1, 8, tile), F32),
-            pltpu.VMEM((groups + 1, HD, tile), F32),
-            pltpu.VMEM((tiles + 1, 2 * tile, LANES), F32),
+            pltpu.VMEM((groups, 8, tile), F32),
+            pltpu.VMEM((groups, HD, tile), F32),
+            pltpu.VMEM((groups, 8, tile), F32),
+            pltpu.VMEM((groups, HD, tile), F32),
+            pltpu.VMEM((tiles, 2 * tile, LANES), F32),
             pltpu.VMEM((slots, rows, LANES), F32),
         ],
         compiler_params=params(VMEM_MOST),

time: 118 us -> 112 us (0.949)
  Pallas kernels: 36.7 us -> 29.6 us
    pallas_call x1, Pallas kernels: 24.1 us -> 17 us  [attention_call(): pl.pallas_call(functools.partial(attention_kernel, pre, place), in_specs=...]
where the time goes in v1:
time: 112 us; the launch traced here: 110 us
  blocking collectives  69.2 us (62%)
  Pallas kernels  29.6 us (26%)
  waiting for transfers between devices  4.71 us (4%)
  starting transfers between devices  4.45 us (4%)
  local copies, waits for them, and re-layouts  1.47 us (1%)
    all_to_all x2, blocking collectives, exchange(): lax.all_to_all(x, AXES, split_axis=0, concat_axis=0, axis_index_groups=sa...  69.2 us
    pallas_call x1, Pallas kernels, attention_call(): pl.pallas_call(functools.partial(attention_kernel, pre, place), in_specs=...  17 us
    pallas_call x1, Pallas kernels, front_call(): pl.pallas_call(front_kernel, in_specs=[smem, vmem, vmem] + [anywhere] * 5...  7.66 us
    pallas_call x1, Pallas kernels, back_call(): pl.pallas_call(back_kernel, in_specs=[smem, vmem, vmem, vmem, vmem], out_...  4.77 us
    ppermute x1, starting transfers between devices, on_device(): before = lax.ppermute(tokens[rows - EDGE:], AXES, up)  3.03 us
  transfers between devices with their start and end apart: 4, of which 3 were waited for; matrix products, arithmetic and copies ran while one was open for 0% of the time, Pallas kernels for 0%

profile of v1, /device:TPU:0, one launch (start us, length us, event | category | flops | bytes accessed | tf_op | source)
XLA Modules:
  0.0 110.2 jit_solution(3636841311953204850)
XLA Ops:
  0.6 0.8 fusion
  1.4 1.3 %collective-permute-start.1 = (bf16[16,1024]{1,0:T(8,128)(2,1)S(1)}, bf16[16,1024]{1,0:T(8,128)(2,1)S(1)}, u32[]{:S(2)}, u32[]{:S(2)}) collective-permute-start(bf16[16,1024]{1,0:T(8,128)(2,1)S(1)} %get-tuple-element.10), channel_id=1, source_target_pairs={{1,0},{2,1},{3,2},{4,3},{5,4},{6,5},{7,6},{8,7},{9,8},{10,9},{11,1... | collective-permute-start | bytes 98312 | tf_op jit(solution)/shard_map/ppermute | solution.py:542
  2.7 3.0 %collective-permute-start = (bf16[16,1024]{1,0:T(8,128)(2,1)S(1)}, bf16[16,1024]{1,0:T(8,128)(2,1)S(1)}, u32[]{:S(2)}, u32[]{:S(2)}) collective-permute-start(bf16[16,1024]{1,0:T(8,128)(2,1)S(1)} %get-tuple-element.11), channel_id=1, source_target_pairs={{0,1},{1,2},{2,3},{3,4},{4,5},{5,6},{6,7},{7,8},{8,9},{9,10},{10,1... | collective-permute-start | bytes 98312 | tf_op jit(solution)/shard_map/ppermute | solution.py:541
  5.7 0.0 collective-permute-done.1.after_ref
  5.7 0.0 copy-start.3
  5.8 0.8 collective-permute-done.before_ref
  6.6 0.0 copy-done.3
  6.6 0.6 copy-done.4
  7.2 7.7 %front.1 = bf16[16,256,128]{2,1,0:T(8,128)(2,1)} custom-call(s32[4]{0:T(128)} %lengths_ref.5, bf16[16,1024]{1,0:T(8,128)(2,1)} %copy-done.4, bf16[16,1024]{1,0:T(8,128)(2,1)} %copy-done.3, bf16[128,1024]{1,0:T(8,128)(2,1)} %x_hbm.1, f32[7,1024]{1,0:T(8,128)} %taps_ref.1, bf16[1024,3072]{1,0:T(8,128)(2,1)} %w_ref.1, bf16[128,1024]{1,0:T(8,128)(2,1)} %cot_hbm.1, ...), custom_call_target="tpu_custom_call" | custom-call | flops 1073741824 | bytes 8388608 | tf_op jit(solution)/shard_map/front/pallas_call | solution.py:152
  14.9 0.0 copy-start.2
  14.9 36.3 %all_to_all.10.qd_ref = bf16[16,256,128]{2,1,0:T(8,128)(2,1)S(1)} all-to-all(bf16[16,256,128]{2,1,0:T(8,128)(2,1)} %front.1), channel_id=1, replica_groups={{0,16,8,24,4,20,12,28,2,18,10,26,6,22,14,30},{1,17,9,25,5,21,13,29,3,19..., dimensions={0} | all-to-all | bytes 2097152 | tf_op jit(solution)/shard_map/all_to_all | solution.py:537
  51.3 0.0 slice-start.1
  51.3 0.1 collective-permute-start.2
  51.4 1.9 %collective-permute-done.2.kv_other = bf16[16,128,128]{2,1,0:T(8,128)(2,1)S(1)} collective-permute-done((bf16[16,128,128]{2,1,0:T(8,128)(2,1)S(1)}, bf16[16,128,128]{2,1,0:T(8,128)(2,1)S(1)}, u32[]{:S(2)}, u32[]{:S(2)}) %collective-permute-start.2) | collective-permute-done | bytes 524320 | tf_op jit(solution)/shard_map/ppermute | solution.py:550
  53.2 0.0 copy-done.2
  53.3 17.0 %attention.1 = (bf16[16,128,128]{2,1,0:T(8,128)(2,1)S(1)}, f32[16,128,128]{2,1,0:T(8,128)S(1)}, f32[16,8,128]{2,1,0:T(8,128)S(1)}, bf16[16,144,128]{2,1,0:T(8,128)(2,1)S(1)}) custom-call(s32[4]{0:T(128)S(1)} %copy-done.2, bf16[16,128,128]{2,1,0:T(8,128)(2,1)S(1)} %slice.12.kv_mine, bf16[16,128,128]{2,1,0:T(8,128)(2,1)S(1)} %collective-permute-done.2.kv_other, ...), custom_call_target="tpu_custom_call" | custom-call | flops 5368709120 | bytes 5242880 | tf_op jit(solution)/shard_map/attention/pallas_call | solution.py:363
  70.2 0.1 collective-permute-start.3
  70.3 2.0 %collective-permute-done.3.got_ref = bf16[16,144,128]{2,1,0:T(8,128)(2,1)S(1)} collective-permute-done((bf16[16,144,128]{2,1,0:T(8,128)(2,1)S(1)}, bf16[16,144,128]{2,1,0:T(8,128)(2,1)S(1)}, u32[]{:S(2)}, u32[]{:S(2)}) %collective-permute-start.3) | collective-permute-done | bytes 589856 | tf_op jit(solution)/shard_map/ppermute | solution.py:552
  72.3 0.2 combine.1
  72.5 32.9 %all_to_all.11.r_ref = bf16[16,272,128]{2,1,0:T(8,128)(2,1)S(1)} all-to-all(bf16[16,272,128]{2,1,0:T(8,128)(2,1)S(1)} %combine.1), channel_id=1, replica_groups={{0,16,8,24,4,20,12,28,2,18,10,26,6,22,14,30},{1,17,9,25,5,21,13,29,3,19..., dimensions={0} | all-to-all | bytes 2228224 | tf_op jit(solution)/shard_map/all_to_all | solution.py:537
  105.4 0.0 slice-done
  105.4 0.0 slice-done.1
  105.4 0.0 copy-done
  105.4 4.8 %back.1 = (bf16[128,1024]{1,0:T(8,128)(2,1)}, bf16[128,1024]{1,0:T(8,128)(2,1)}) custom-call(s32[4]{0:T(128)S(1)} %copy-done.2, bf16[16,272,128]{2,1,0:T(8,128)(2,1)S(1)} %all_to_all.11.r_ref, f32[7,1024]{1,0:T(8,128)S(1)} %copy-done.1, bf16[1024,3072]{1,0:T(8,128)(2,1)S(1)} %bitcast.1, bf16[1024,1024]{1,0:T(8,128)(2,1)S(1)} %copy-done), custom_call_target="tpu_custom_call" | custom-call | flops 1073741824 | bytes 8388608 | tf_op jit(solution)/shard_map/back/pallas_call | solution.py:494
  (7 shorter events, 0.0 us)
Async XLA Ops:
  1.4 4.3 %collective-permute-start.1 = (bf16[16,1024]{1,0:T(8,128)(2,1)S(1)}, bf16[16,1024]{1,0:T(8,128)(2,1)S(1)}, u32[]{:S(2)}, u32[]{:S(2)}) collective-permute-start(bf16[16,1024]{1,0:T(8,128)(2,1)S(1)} %get-tuple-element.10), channel_id=1, source_target_pairs={{1,0},{2,1},{3,2},{4,3},{5,4},{6,5},{7,6},{8,7},{9,8},{10,9},{11,1... | collective-permute-start | bytes 98312 | tf_op jit(solution)/shard_map/ppermute | solution.py:542
  2.7 3.9 %collective-permute-start = (bf16[16,1024]{1,0:T(8,128)(2,1)S(1)}, bf16[16,1024]{1,0:T(8,128)(2,1)S(1)}, u32[]{:S(2)}, u32[]{:S(2)}) collective-permute-start(bf16[16,1024]{1,0:T(8,128)(2,1)S(1)} %get-tuple-element.11), channel_id=1, source_target_pairs={{0,1},{1,2},{2,3},{3,4},{4,5},{5,6},{6,7},{7,8},{8,9},{9,10},{10,1... | collective-permute-start | bytes 98312 | tf_op jit(solution)/shard_map/ppermute | solution.py:541
  5.7 0.8 copy-start.3
  6.6 0.6 copy-start.4
  14.9 38.4 %copy-start.2 = (s32[4]{0:T(128)S(1)}, s32[4]{0:T(128)}, u32[]{:S(2)}) copy-start(s32[4]{0:T(128)} %lengths_ref.5) | copy-start | bytes 52
  51.2 54.2 %slice-start = ((s8[6291456]{0:T(1024)(128)(4,1)}), s8[4194304]{0:T(1024)(128)(4,1)S(1)}, s32[]{:S(2)}) async-start(s8[6291456]{0:T(1024)(128)(4,1)} %bitcast), calls=%async_computation.2 | async-start | bytes 8388608
  51.3 54.1 %slice-start.1 = ((s8[6291456]{0:T(1024)(128)(4,1)}), s8[2097152]{0:T(1024)(128)(4,1)S(1)}, s32[]{:S(2)}) async-start(s8[6291456]{0:T(1024)(128)(4,1)} %bitcast), calls=%async_computation.3 | async-start | bytes 4194304
  51.3 2.0 %collective-permute-start.2 = (bf16[16,128,128]{2,1,0:T(8,128)(2,1)S(1)}, bf16[16,128,128]{2,1,0:T(8,128)(2,1)S(1)}, u32[]{:S(2)}, u32[]{:S(2)}) collective-permute-start(bf16[16,128,128]{2,1,0:T(8,128)(2,1)S(1)} %slice.12.kv_mine), channel_id=1, source_target_pairs={{0,1},{1,0},{2,3},{3,2},{4,5},{5,4},{6,7},{7,6},{8,9},{9,8},{10,11... | collective-permute-start | bytes 1572872 | tf_op jit(solution)/shard_map/ppermute | solution.py:550
  70.2 2.1 %collective-permute-start.3 = (bf16[16,144,128]{2,1,0:T(8,128)(2,1)S(1)}, bf16[16,144,128]{2,1,0:T(8,128)(2,1)S(1)}, u32[]{:S(2)}, u32[]{:S(2)}) collective-permute-start(bf16[16,144,128]{2,1,0:T(8,128)(2,1)S(1)} %get-tuple-element.9), channel_id=1, source_target_pairs={{0,1},{1,0},{2,3},{3,2},{4,5},{5,4},{6,7},{7,6},{8,9},{9,8},{10,11... | collective-permute-start | bytes 1769480 | tf_op jit(solution)/shard_map/ppermute | solution.py:552
  72.3 33.1 %copy-start = (bf16[1024,1024]{1,0:T(8,128)(2,1)S(1)}, bf16[1024,1024]{1,0:T(8,128)(2,1)}, u32[]{:S(2)}) copy-start(bf16[1024,1024]{1,0:T(8,128)(2,1)} %wo_ref.1) | copy-start | bytes 6291460
  72.3 33.1 %copy-start.1 = (f32[7,1024]{1,0:T(8,128)S(1)}, f32[7,1024]{1,0:T(8,128)}, u32[]{:S(2)}) copy-start(f32[7,1024]{1,0:T(8,128)} %taps_ref.1) | copy-start | bytes 86020

commit v2 on v1

--- a/solution.py
+++ b/solution.py
@@ -19,7 +19,7 @@
 FAR = -1e30
 FRONT_STEPS = 4
 BACK_STEPS = 4
-VMEM_ALL = 60 * 1024 * 1024
+VMEM_ALL = 57_500_000
 VMEM_MOST = 44 * 1024 * 1024
 VMEM_SOME = 24 * 1024 * 1024
 F32 = jnp.float32
@@ -82,7 +82,7 @@
 
 
 def front_kernel(
-    lengths_ref, before_ref, after_ref, x_hbm, taps_hbm, w_hbm, cot_hbm, wo_hbm,
+    lengths_ref, inner_ref, outer_ref, x_hbm, taps_hbm, w_hbm, cot_hbm, wo_hbm,
     out_ref, x_ref, taps_ref, w_ref, cot_ref, wo_ref, padded, projected, d_rows, sems,
 ):
     rows, width = x_ref.shape
@@ -112,8 +112,10 @@
     for pair in parts:
         for c in pair:
             c.start()
-    padded[pl.ds(0, 8), :] = before_ref[...].astype(F32)[EDGE - 8 :]
-    padded[pl.ds(8 + rows, 8), :] = after_ref[...].astype(F32)[:8]
+    even = device_index() % 2 == 0
+    inner, outer = inner_ref[...].astype(F32), outer_ref[...].astype(F32)
+    padded[pl.ds(0, 8), :] = jnp.where(even, outer[EDGE - 8 :], inner[EDGE - 8 :])
+    padded[pl.ds(8 + rows, 8), :] = jnp.where(even, inner[:8], outer[:8])
     for c in whole:
         c.wait()
     padded[pl.ds(8, rows), :] = x_ref[...].astype(F32)
@@ -143,7 +145,7 @@
         out_ref[2 * pair + 1] = jnp.concatenate([zip_high(k, v), zip_high(q, d)]).astype(BF16)
 
 
-def front_call(lengths, before, x, after, taps, w_qkv, cotangent, w_out):
+def front_call(lengths, inner, outer, x, taps, w_qkv, cotangent, w_out):
     rows, width = x.shape
     heads = width // HD
     smem = pl.BlockSpec(memory_space=pltpu.SMEM)
@@ -170,7 +172,7 @@
             flops=8 * rows * width * width, bytes_accessed=8 * width * width, transcendentals=0
         ),
         name="front",
-    )(lengths, before, after, x, taps, w_qkv, cotangent, w_out)
+    )(lengths, inner, outer, x, taps, w_qkv, cotangent, w_out)
 
 
 def attention_kernel(
@@ -530,17 +532,18 @@
         for side in range(2)
     ]
     swapped = [(i, i ^ 1) for i in range(devices)]
-    up = [(i, i + 1) for i in range(devices - 1)]
-    down = [(i + 1, i) for i in range(devices - 1)]
+    across = [(i, i + (1 if i % 2 else -1)) for i in range(1, devices - 1)]
 
     def exchange(x):
         return lax.all_to_all(
             x, AXES, split_axis=0, concat_axis=0, axis_index_groups=same_side, tiled=True
         )
 
-    before = lax.ppermute(tokens[rows - EDGE :], AXES, up)
-    after = lax.ppermute(tokens[:EDGE], AXES, down)
-    sent = front_call(lengths, before, tokens, after, conv_kernel, w_qkv, cotangent, w_out)
+    first, last = tokens[:EDGE], tokens[rows - EDGE :]
+    even = me % 2 == 0
+    inner = lax.ppermute(jnp.where(even, last, first), AXES, swapped)
+    outer = lax.ppermute(jnp.where(even, first, last), AXES, across)
+    sent = front_call(lengths, inner, outer, tokens, conv_kernel, w_qkv, cotangent, w_out)
     qd = exchange(sent)
     kv_mine = qd[:, :rows]
     if pre:

time: 112 us -> 112 us (level)
  Pallas kernels: 29.6 us -> 31.4 us
  blocking collectives: 69.2 us -> 67.8 us
    pallas_call x1, Pallas kernels: 17 us -> 18.8 us  [attention_call(): pl.pallas_call(functools.partial(attention_kernel, pre, place), in_specs=...]
    all_to_all x2, blocking collectives: 69.2 us -> 67.8 us  [exchange(): lax.all_to_all(x, AXES, split_axis=0, concat_axis=0, axis_index_groups=sa...]
where the time goes in v2:
time: 112 us; the launch traced here: 111 us
  blocking collectives  67.8 us (61%)
  Pallas kernels  31.4 us (28%)
  starting transfers between devices  5.29 us (5%)
  waiting for transfers between devices  4.62 us (4%)
    all_to_all x2, blocking collectives, exchange(): lax.all_to_all(x, AXES, split_axis=0, concat_axis=0, axis_index_groups=sa...  67.8 us
    pallas_call x1, Pallas kernels, attention_call(): pl.pallas_call(functools.partial(attention_kernel, pre, place), in_specs=...  18.8 us
    pallas_call x1, Pallas kernels, front_call(): pl.pallas_call(front_kernel, in_specs=[smem, vmem, vmem] + [anywhere] * 5...  7.67 us
    pallas_call x1, Pallas kernels, back_call(): pl.pallas_call(back_kernel, in_specs=[smem, vmem, vmem, vmem, vmem], out_...  4.76 us
    ppermute x1, starting transfers between devices, on_device(): inner = lax.ppermute(jnp.where(even, last, first), AXES, swapped)  4.36 us
  transfers between devices with their start and end apart: 4, of which 3 were waited for; matrix products, arithmetic and copies ran while one was open for 0% of the time, Pallas kernels for 0%

profile of v2, /device:TPU:0, one launch (start us, length us, event | category | flops | bytes accessed | tf_op | source)
XLA Modules:
  0.0 111.3 jit_solution(9422233036373085556)
XLA Ops:
  0.6 0.8 broadcast_select_fusion
  1.4 0.7 collective-permute-start.1
  2.1 4.4 %collective-permute-start = (bf16[16,1024]{1,0:T(8,128)(2,1)S(1)}, bf16[16,1024]{1,0:T(8,128)(2,1)S(1)}, u32[]{:S(2)}, u32[]{:S(2)}) collective-permute-start(bf16[16,1024]{1,0:T(8,128)(2,1)S(1)} %get-tuple-element.11), channel_id=1, source_target_pairs={{0,1},{1,0},{2,3},{3,2},{4,5},{5,4},{6,7},{7,6},{8,9},{9,8},{10,11... | collective-permute-start | bytes 98312 | tf_op jit(solution)/shard_map/ppermute | solution.py:544
  6.5 0.0 collective-permute-done.1.outer_ref
  6.5 0.9 collective-permute-done.inner_ref
  7.3 0.0 copy-done.3
  7.3 0.6 copy-done.4
  7.9 7.7 %front.1 = bf16[16,256,128]{2,1,0:T(8,128)(2,1)} custom-call(s32[4]{0:T(128)} %lengths_ref.5, bf16[16,1024]{1,0:T(8,128)(2,1)} %copy-done.4, bf16[16,1024]{1,0:T(8,128)(2,1)} %copy-done.3, bf16[128,1024]{1,0:T(8,128)(2,1)} %x_hbm.1, f32[7,1024]{1,0:T(8,128)} %taps_ref.1, bf16[1024,3072]{1,0:T(8,128)(2,1)} %w_ref.1, bf16[128,1024]{1,0:T(8,128)(2,1)} %cot_hbm.1, ...), custom_call_target="tpu_custom_call" | custom-call | flops 1073741824 | bytes 8388608 | tf_op jit(solution)/shard_map/front/pallas_call | solution.py:154
  15.6 0.0 copy-start.2
  15.6 34.9 %all_to_all.10.qd_ref = bf16[16,256,128]{2,1,0:T(8,128)(2,1)S(1)} all-to-all(bf16[16,256,128]{2,1,0:T(8,128)(2,1)} %front.1), channel_id=1, replica_groups={{0,16,8,24,4,20,12,28,2,18,10,26,6,22,14,30},{1,17,9,25,5,21,13,29,3,19..., dimensions={0} | all-to-all | bytes 2097152 | tf_op jit(solution)/shard_map/all_to_all | solution.py:538
  50.6 0.0 slice-start.1
  50.6 0.1 collective-permute-start.2
  50.6 1.9 %collective-permute-done.2.kv_other = bf16[16,128,128]{2,1,0:T(8,128)(2,1)S(1)} collective-permute-done((bf16[16,128,128]{2,1,0:T(8,128)(2,1)S(1)}, bf16[16,128,128]{2,1,0:T(8,128)(2,1)S(1)}, u32[]{:S(2)}, u32[]{:S(2)}) %collective-permute-start.2) | collective-permute-done | bytes 524320 | tf_op jit(solution)/shard_map/ppermute | solution.py:553
  52.5 0.0 copy-done.2
  52.5 18.8 %attention.1 = (bf16[16,128,128]{2,1,0:T(8,128)(2,1)S(1)}, f32[16,128,128]{2,1,0:T(8,128)S(1)}, f32[16,8,128]{2,1,0:T(8,128)S(1)}, bf16[16,144,128]{2,1,0:T(8,128)(2,1)S(1)}) custom-call(s32[4]{0:T(128)S(1)} %copy-done.2, bf16[16,128,128]{2,1,0:T(8,128)(2,1)S(1)} %slice.12.kv_mine, bf16[16,128,128]{2,1,0:T(8,128)(2,1)S(1)} %collective-permute-done.2.kv_other, ...), custom_call_target="tpu_custom_call" | custom-call | flops 5368709120 | bytes 5242880 | tf_op jit(solution)/shard_map/attention/pallas_call | solution.py:365
  71.3 0.2 collective-permute-start.3
  71.5 1.9 %collective-permute-done.3.got_ref = bf16[16,144,128]{2,1,0:T(8,128)(2,1)S(1)} collective-permute-done((bf16[16,144,128]{2,1,0:T(8,128)(2,1)S(1)}, bf16[16,144,128]{2,1,0:T(8,128)(2,1)S(1)}, u32[]{:S(2)}, u32[]{:S(2)}) %collective-permute-start.3) | collective-permute-done | bytes 589856 | tf_op jit(solution)/shard_map/ppermute | solution.py:555
  73.4 0.2 combine.1
  73.6 32.9 %all_to_all.11.r_ref = bf16[16,272,128]{2,1,0:T(8,128)(2,1)S(1)} all-to-all(bf16[16,272,128]{2,1,0:T(8,128)(2,1)S(1)} %combine.1), channel_id=1, replica_groups={{0,16,8,24,4,20,12,28,2,18,10,26,6,22,14,30},{1,17,9,25,5,21,13,29,3,19..., dimensions={0} | all-to-all | bytes 2228224 | tf_op jit(solution)/shard_map/all_to_all | solution.py:538
  106.5 0.0 slice-done
  106.5 0.0 slice-done.1
  106.5 0.0 copy-done
  106.5 0.0 copy-done.1
  106.5 4.8 %back.1 = (bf16[128,1024]{1,0:T(8,128)(2,1)}, bf16[128,1024]{1,0:T(8,128)(2,1)}) custom-call(s32[4]{0:T(128)S(1)} %copy-done.2, bf16[16,272,128]{2,1,0:T(8,128)(2,1)S(1)} %all_to_all.11.r_ref, f32[7,1024]{1,0:T(8,128)S(1)} %copy-done.1, bf16[1024,3072]{1,0:T(8,128)(2,1)S(1)} %bitcast.1, bf16[1024,1024]{1,0:T(8,128)(2,1)S(1)} %copy-done), custom_call_target="tpu_custom_call" | custom-call | flops 1073741824 | bytes 8388608 | tf_op jit(solution)/shard_map/back/pallas_call | solution.py:496
  (7 shorter events, 0.0 us)
Async XLA Ops:
  1.4 5.0 %collective-permute-start.1 = (bf16[16,1024]{1,0:T(8,128)(2,1)S(1)}, bf16[16,1024]{1,0:T(8,128)(2,1)S(1)}, u32[]{:S(2)}, u32[]{:S(2)}) collective-permute-start(bf16[16,1024]{1,0:T(8,128)(2,1)S(1)} %get-tuple-element.10), channel_id=1, source_target_pairs={{1,2},{2,1},{3,4},{4,3},{5,6},{6,5},{7,8},{8,7},{9,10},{10,9},{11,... | collective-permute-start | bytes 98312 | tf_op jit(solution)/shard_map/ppermute | solution.py:545
  2.1 5.2 %collective-permute-start = (bf16[16,1024]{1,0:T(8,128)(2,1)S(1)}, bf16[16,1024]{1,0:T(8,128)(2,1)S(1)}, u32[]{:S(2)}, u32[]{:S(2)}) collective-permute-start(bf16[16,1024]{1,0:T(8,128)(2,1)S(1)} %get-tuple-element.11), channel_id=1, source_target_pairs={{0,1},{1,0},{2,3},{3,2},{4,5},{5,4},{6,7},{7,6},{8,9},{9,8},{10,11... | collective-permute-start | bytes 98312 | tf_op jit(solution)/shard_map/ppermute | solution.py:544
  6.5 0.9 copy-start.3
  7.3 0.6 copy-start.4
  15.6 36.9 %copy-start.2 = (s32[4]{0:T(128)S(1)}, s32[4]{0:T(128)}, u32[]{:S(2)}) copy-start(s32[4]{0:T(128)} %lengths_ref.5) | copy-start | bytes 52
  50.5 56.0 %slice-start = ((s8[6291456]{0:T(1024)(128)(4,1)}), s8[4194304]{0:T(1024)(128)(4,1)S(1)}, s32[]{:S(2)}) async-start(s8[6291456]{0:T(1024)(128)(4,1)} %bitcast), calls=%async_computation.2 | async-start | bytes 8388608
  50.6 55.9 %slice-start.1 = ((s8[6291456]{0:T(1024)(128)(4,1)}), s8[2097152]{0:T(1024)(128)(4,1)S(1)}, s32[]{:S(2)}) async-start(s8[6291456]{0:T(1024)(128)(4,1)} %bitcast), calls=%async_computation.3 | async-start | bytes 4194304
  50.6 2.0 %collective-permute-start.2 = (bf16[16,128,128]{2,1,0:T(8,128)(2,1)S(1)}, bf16[16,128,128]{2,1,0:T(8,128)(2,1)S(1)}, u32[]{:S(2)}, u32[]{:S(2)}) collective-permute-start(bf16[16,128,128]{2,1,0:T(8,128)(2,1)S(1)} %slice.12.kv_mine), channel_id=1, source_target_pairs={{0,1},{1,0},{2,3},{3,2},{4,5},{5,4},{6,7},{7,6},{8,9},{9,8},{10,11... | collective-permute-start | bytes 1572872 | tf_op jit(solution)/shard_map/ppermute | solution.py:553
  71.3 2.1 %collective-permute-start.3 = (bf16[16,144,128]{2,1,0:T(8,128)(2,1)S(1)}, bf16[16,144,128]{2,1,0:T(8,128)(2,1)S(1)}, u32[]{:S(2)}, u32[]{:S(2)}) collective-permute-start(bf16[16,144,128]{2,1,0:T(8,128)(2,1)S(1)} %get-tuple-element.9), channel_id=1, source_target_pairs={{0,1},{1,0},{2,3},{3,2},{4,5},{5,4},{6,7},{7,6},{8,9},{9,8},{10,11... | collective-permute-start | bytes 1769480 | tf_op jit(solution)/shard_map/ppermute | solution.py:555
  73.4 33.1 %copy-start = (bf16[1024,1024]{1,0:T(8,128)(2,1)S(1)}, bf16[1024,1024]{1,0:T(8,128)(2,1)}, u32[]{:S(2)}) copy-start(bf16[1024,1024]{1,0:T(8,128)(2,1)} %wo_ref.1) | copy-start | bytes 6291460
  73.4 33.1 %copy-start.1 = (f32[7,1024]{1,0:T(8,128)S(1)}, f32[7,1024]{1,0:T(8,128)}, u32[]{:S(2)}) copy-start(f32[7,1024]{1,0:T(8,128)} %taps_ref.1) | copy-start | bytes 86020

commit v3 on v2

--- a/solution.py
+++ b/solution.py
@@ -206,8 +206,6 @@
 
     count = jnp.int32(groups)
     for u in range(groups):
-        visit_q[u] = u
-        visit_k[u] = u + pre // 2
         first = base + u * (2 * tile) + parity * rows
         begin, end = jnp.int32(0), jnp.int32(0)
         for i in range(lengths_ref.shape[0]):
@@ -234,8 +232,8 @@
                 pos = origin + row_at(2 * t + i, side)
                 mark = jnp.where((pos >= starts) & (pos < stops), 0.0, FAR)
                 marked_ref[t, at] = jnp.where(low, block.astype(F32), mark).astype(BF16)
-    for ref in (acc_ref, total_ref, context_ref, d_query_ref):
-        ref[...] = jnp.zeros_like(ref)
+    for t in range(pre // 2):
+        acc_ref[t] = jnp.zeros_like(acc_ref[t])
     for u in range(groups):
         for i in range(2):
             qd = qd_ref[place(2 * u + i, 0), pl.ds(rows, rows)]
@@ -256,35 +254,37 @@
     side = jnp.where(k_sub < tile, parity, 1 - parity)
     causal = k_sub // rows % 2 * tile + k_sub % rows + side * rows <= q_row
 
-    def forward(i, diagonal):
-        u, t = visit_q[i], visit_k[i]
+    def forward(i, u, t, diagonal):
         scores = lax.dot_general(marked_ref[t], query_ref[u], nt, preferred_element_type=F32)
         e = jnp.exp2(scores * to_exp2)
         if diagonal:
             e = jnp.where(causal, e, 0.0)
         e_ref[i] = e
         context = jnp.dot(turned_ref[t, HD:], e.astype(BF16), preferred_element_type=F32)
-        return u, jnp.sum(e.reshape(2 * tile // 8, 8, tile), axis=0), context
-
-    def forward_some(diagonal, first, per):
+        return jnp.sum(e.reshape(2 * tile // 8, 8, tile), axis=0), context
+
+    def forward_some(first, per):
         def run(j, carry):
-            for u, total, context in [
-                forward(first + per * j + i, diagonal) for i in range(per)
-            ]:
+            at = [first + per * j + i for i in range(per)]
+            groups_at = [visit_q[i] for i in at]
+            parts = [forward(i, u, visit_k[i], False) for i, u in zip(at, groups_at)]
+            for u, (total, context) in zip(groups_at, parts):
                 total_ref[u] += total
                 context_ref[u] += context
             return carry
 
         return run
 
-    def run_all(make, first, last):
-        steps = (last - first) // PER_STEP
-        lax.fori_loop(0, steps, make(first, PER_STEP), 0)
-        rest = first + steps * PER_STEP
-        lax.fori_loop(0, last - rest, make(rest, 1), 0)
-
-    lax.fori_loop(0, groups // PER_STEP, forward_some(True, 0, PER_STEP), 0)
-    run_all(functools.partial(forward_some, False), groups, count)
+    def run_rest(make):
+        first = groups
+        for per in (PER_STEP, 2, 1):
+            steps = (count - first) // per
+            lax.fori_loop(0, steps, make(first, per), 0)
+            first = first + steps * per
+
+    for u in range(groups):
+        total_ref[u], context_ref[u] = forward(u, u, u + pre // 2, True)
+    run_rest(forward_some)
     for u in range(groups):
         inverse = 1.0 / jnp.sum(total_ref[u], axis=0, keepdims=True)
         context = (context_ref[u] * inverse).astype(BF16).astype(F32)
@@ -292,8 +292,7 @@
         row_ref[u, pl.ds(0, 1)] = inverse
         row_ref[u, pl.ds(1, 1)] = jnp.sum(d_turned_ref[u] * context, axis=0, keepdims=True)
 
-    def backward(i):
-        u, t = visit_q[i], visit_k[i]
+    def backward(i, u, t):
         row = row_ref[u]
         probs = e_ref[i] * row[0:1]
         d_probs = lax.dot_general(
@@ -303,20 +302,22 @@
         both = jnp.concatenate([d_scores, probs.astype(BF16)], axis=1)
         d_keys = jnp.dot(both, qd_cat_ref[u], preferred_element_type=F32)
         d_queries = jnp.dot(turned_ref[t, :HD], d_scores, preferred_element_type=F32)
-        return u, t, d_keys, d_queries
+        return d_keys, d_queries
 
     def backward_some(first, per):
         def run(j, carry):
-            for u, t, d_keys, d_queries in [
-                backward(first + per * j + i) for i in range(per)
-            ]:
+            at = [(i, visit_q[i], visit_k[i]) for i in (first + per * j + i for i in range(per))]
+            parts = [backward(i, u, t) for i, u, t in at]
+            for (_, u, t), (d_keys, d_queries) in zip(at, parts):
                 acc_ref[t] += d_keys
                 d_query_ref[u] += d_queries
             return carry
 
         return run
 
-    run_all(backward_some, 0, count)
+    for u in range(groups):
+        acc_ref[u + pre // 2], d_query_ref[u] = backward(u, u, u + pre // 2)
+    run_rest(backward_some)
     for u in range(groups):
         packed = jnp.concatenate([context_ref[u], d_query_ref[u] * unit], axis=0).T
         for i in range(2):

time: 112 us -> 110 us (0.982)
  Pallas kernels: 31.4 us -> 29.6 us
    pallas_call x1, Pallas kernels: 18.8 us -> 17 us  [attention_call(): pl.pallas_call(functools.partial(attention_kernel, pre, place), in_specs=...]
where the time goes in v3:
time: 110 us; the launch traced here: 109 us
  blocking collectives  67.8 us (62%)
  Pallas kernels  29.6 us (27%)
  starting transfers between devices  5.29 us (5%)
  waiting for transfers between devices  4.62 us (4%)
    all_to_all x2, blocking collectives, exchange(): lax.all_to_all(x, AXES, split_axis=0, concat_axis=0, axis_index_groups=sa...  67.8 us
    pallas_call x1, Pallas kernels, attention_call(): pl.pallas_call(functools.partial(attention_kernel, pre, place), in_specs=...  17 us
    pallas_call x1, Pallas kernels, front_call(): pl.pallas_call(front_kernel, in_specs=[smem, vmem, vmem] + [anywhere] * 5...  7.67 us
    pallas_call x1, Pallas kernels, back_call(): pl.pallas_call(back_kernel, in_specs=[smem, vmem, vmem, vmem, vmem], out_...  4.77 us
    ppermute x1, starting transfers between devices, on_device(): inner = lax.ppermute(jnp.where(even, last, first), AXES, swapped)  4.36 us
  transfers between devices with their start and end apart: 4, of which 3 were waited for; matrix products, arithmetic and copies ran while one was open for 0% of the time, Pallas kernels for 0%

profile of v3, /device:TPU:0, one launch (start us, length us, event | category | flops | bytes accessed | tf_op | source)
XLA Modules:
  0.0 109.5 jit_solution(11524010644978275800)
XLA Ops:
  0.6 0.8 broadcast_select_fusion
  1.4 0.7 collective-permute-start.1
  2.1 4.4 %collective-permute-start = (bf16[16,1024]{1,0:T(8,128)(2,1)S(1)}, bf16[16,1024]{1,0:T(8,128)(2,1)S(1)}, u32[]{:S(2)}, u32[]{:S(2)}) collective-permute-start(bf16[16,1024]{1,0:T(8,128)(2,1)S(1)} %get-tuple-element.11), channel_id=1, source_target_pairs={{0,1},{1,0},{2,3},{3,2},{4,5},{5,4},{6,7},{7,6},{8,9},{9,8},{10,11... | collective-permute-start | bytes 98312 | tf_op jit(solution)/shard_map/ppermute | solution.py:545
  6.5 0.0 collective-permute-done.1.outer_ref
  6.5 0.9 collective-permute-done.inner_ref
  7.3 0.0 copy-done.3
  7.3 0.6 copy-done.4
  7.9 7.7 %front.1 = bf16[16,256,128]{2,1,0:T(8,128)(2,1)} custom-call(s32[4]{0:T(128)} %lengths_ref.5, bf16[16,1024]{1,0:T(8,128)(2,1)} %copy-done.4, bf16[16,1024]{1,0:T(8,128)(2,1)} %copy-done.3, bf16[128,1024]{1,0:T(8,128)(2,1)} %x_hbm.1, f32[7,1024]{1,0:T(8,128)} %taps_ref.1, bf16[1024,3072]{1,0:T(8,128)(2,1)} %w_ref.1, bf16[128,1024]{1,0:T(8,128)(2,1)} %cot_hbm.1, ...), custom_call_target="tpu_custom_call" | custom-call | flops 1073741824 | bytes 8388608 | tf_op jit(solution)/shard_map/front/pallas_call | solution.py:154
  15.6 0.0 copy-start.2
  15.6 34.9 %all_to_all.10.qd_ref = bf16[16,256,128]{2,1,0:T(8,128)(2,1)S(1)} all-to-all(bf16[16,256,128]{2,1,0:T(8,128)(2,1)} %front.1), channel_id=1, replica_groups={{0,16,8,24,4,20,12,28,2,18,10,26,6,22,14,30},{1,17,9,25,5,21,13,29,3,19..., dimensions={0} | all-to-all | bytes 2097152 | tf_op jit(solution)/shard_map/all_to_all | solution.py:539
  50.6 0.0 slice-start.1
  50.6 0.1 collective-permute-start.2
  50.6 1.9 %collective-permute-done.2.kv_other = bf16[16,128,128]{2,1,0:T(8,128)(2,1)S(1)} collective-permute-done((bf16[16,128,128]{2,1,0:T(8,128)(2,1)S(1)}, bf16[16,128,128]{2,1,0:T(8,128)(2,1)S(1)}, u32[]{:S(2)}, u32[]{:S(2)}) %collective-permute-start.2) | collective-permute-done | bytes 524320 | tf_op jit(solution)/shard_map/ppermute | solution.py:554
  52.5 0.0 copy-done.2
  52.5 17.0 %attention.1 = (bf16[16,128,128]{2,1,0:T(8,128)(2,1)S(1)}, f32[16,128,128]{2,1,0:T(8,128)S(1)}, f32[16,8,128]{2,1,0:T(8,128)S(1)}, bf16[16,144,128]{2,1,0:T(8,128)(2,1)S(1)}) custom-call(s32[4]{0:T(128)S(1)} %copy-done.2, bf16[16,128,128]{2,1,0:T(8,128)(2,1)S(1)} %slice.12.kv_mine, bf16[16,128,128]{2,1,0:T(8,128)(2,1)S(1)} %collective-permute-done.2.kv_other, ...), custom_call_target="tpu_custom_call" | custom-call | flops 5368709120 | bytes 5242880 | tf_op jit(solution)/shard_map/attention/pallas_call | solution.py:366
  69.5 0.2 collective-permute-start.3
  69.7 1.9 %collective-permute-done.3.got_ref = bf16[16,144,128]{2,1,0:T(8,128)(2,1)S(1)} collective-permute-done((bf16[16,144,128]{2,1,0:T(8,128)(2,1)S(1)}, bf16[16,144,128]{2,1,0:T(8,128)(2,1)S(1)}, u32[]{:S(2)}, u32[]{:S(2)}) %collective-permute-start.3) | collective-permute-done | bytes 589856 | tf_op jit(solution)/shard_map/ppermute | solution.py:556
  71.6 0.2 combine.1
  71.8 32.9 %all_to_all.11.r_ref = bf16[16,272,128]{2,1,0:T(8,128)(2,1)S(1)} all-to-all(bf16[16,272,128]{2,1,0:T(8,128)(2,1)S(1)} %combine.1), channel_id=1, replica_groups={{0,16,8,24,4,20,12,28,2,18,10,26,6,22,14,30},{1,17,9,25,5,21,13,29,3,19..., dimensions={0} | all-to-all | bytes 2228224 | tf_op jit(solution)/shard_map/all_to_all | solution.py:539
  104.7 0.0 slice-done
  104.7 0.0 slice-done.1
  104.7 0.0 copy-done
  104.7 0.0 copy-done.1
  104.7 4.8 %back.1 = (bf16[128,1024]{1,0:T(8,128)(2,1)}, bf16[128,1024]{1,0:T(8,128)(2,1)}) custom-call(s32[4]{0:T(128)S(1)} %copy-done.2, bf16[16,272,128]{2,1,0:T(8,128)(2,1)S(1)} %all_to_all.11.r_ref, f32[7,1024]{1,0:T(8,128)S(1)} %copy-done.1, bf16[1024,3072]{1,0:T(8,128)(2,1)S(1)} %bitcast.1, bf16[1024,1024]{1,0:T(8,128)(2,1)S(1)} %copy-done), custom_call_target="tpu_custom_call" | custom-call | flops 1073741824 | bytes 8388608 | tf_op jit(solution)/shard_map/back/pallas_call | solution.py:497
  (7 shorter events, 0.0 us)
Async XLA Ops:
  1.4 5.0 %collective-permute-start.1 = (bf16[16,1024]{1,0:T(8,128)(2,1)S(1)}, bf16[16,1024]{1,0:T(8,128)(2,1)S(1)}, u32[]{:S(2)}, u32[]{:S(2)}) collective-permute-start(bf16[16,1024]{1,0:T(8,128)(2,1)S(1)} %get-tuple-element.10), channel_id=1, source_target_pairs={{1,2},{2,1},{3,4},{4,3},{5,6},{6,5},{7,8},{8,7},{9,10},{10,9},{11,... | collective-permute-start | bytes 98312 | tf_op jit(solution)/shard_map/ppermute | solution.py:546
  2.1 5.2 %collective-permute-start = (bf16[16,1024]{1,0:T(8,128)(2,1)S(1)}, bf16[16,1024]{1,0:T(8,128)(2,1)S(1)}, u32[]{:S(2)}, u32[]{:S(2)}) collective-permute-start(bf16[16,1024]{1,0:T(8,128)(2,1)S(1)} %get-tuple-element.11), channel_id=1, source_target_pairs={{0,1},{1,0},{2,3},{3,2},{4,5},{5,4},{6,7},{7,6},{8,9},{9,8},{10,11... | collective-permute-start | bytes 98312 | tf_op jit(solution)/shard_map/ppermute | solution.py:545
  6.5 0.9 copy-start.3
  7.3 0.6 copy-start.4
  15.6 36.9 %copy-start.2 = (s32[4]{0:T(128)S(1)}, s32[4]{0:T(128)}, u32[]{:S(2)}) copy-start(s32[4]{0:T(128)} %lengths_ref.5) | copy-start | bytes 52
  50.5 54.2 %slice-start = ((s8[6291456]{0:T(1024)(128)(4,1)}), s8[4194304]{0:T(1024)(128)(4,1)S(1)}, s32[]{:S(2)}) async-start(s8[6291456]{0:T(1024)(128)(4,1)} %bitcast), calls=%async_computation.2 | async-start | bytes 8388608
  50.6 54.1 %slice-start.1 = ((s8[6291456]{0:T(1024)(128)(4,1)}), s8[2097152]{0:T(1024)(128)(4,1)S(1)}, s32[]{:S(2)}) async-start(s8[6291456]{0:T(1024)(128)(4,1)} %bitcast), calls=%async_computation.3 | async-start | bytes 4194304
  50.6 2.0 %collective-permute-start.2 = (bf16[16,128,128]{2,1,0:T(8,128)(2,1)S(1)}, bf16[16,128,128]{2,1,0:T(8,128)(2,1)S(1)}, u32[]{:S(2)}, u32[]{:S(2)}) collective-permute-start(bf16[16,128,128]{2,1,0:T(8,128)(2,1)S(1)} %slice.12.kv_mine), channel_id=1, source_target_pairs={{0,1},{1,0},{2,3},{3,2},{4,5},{5,4},{6,7},{7,6},{8,9},{9,8},{10,11... | collective-permute-start | bytes 1572872 | tf_op jit(solution)/shard_map/ppermute | solution.py:554
  69.5 2.1 %collective-permute-start.3 = (bf16[16,144,128]{2,1,0:T(8,128)(2,1)S(1)}, bf16[16,144,128]{2,1,0:T(8,128)(2,1)S(1)}, u32[]{:S(2)}, u32[]{:S(2)}) collective-permute-start(bf16[16,144,128]{2,1,0:T(8,128)(2,1)S(1)} %get-tuple-element.9), channel_id=1, source_target_pairs={{0,1},{1,0},{2,3},{3,2},{4,5},{5,4},{6,7},{7,6},{8,9},{9,8},{10,11... | collective-permute-start | bytes 1769480 | tf_op jit(solution)/shard_map/ppermute | solution.py:556
  71.6 33.1 %copy-start = (bf16[1024,1024]{1,0:T(8,128)(2,1)S(1)}, bf16[1024,1024]{1,0:T(8,128)(2,1)}, u32[]{:S(2)}) copy-start(bf16[1024,1024]{1,0:T(8,128)(2,1)} %wo_ref.1) | copy-start | bytes 6291460
  71.6 33.1 %copy-start.1 = (f32[7,1024]{1,0:T(8,128)S(1)}, f32[7,1024]{1,0:T(8,128)}, u32[]{:S(2)}) copy-start(f32[7,1024]{1,0:T(8,128)} %taps_ref.1) | copy-start | bytes 86020

commit v4 on v3

--- a/solution.py
+++ b/solution.py
@@ -15,7 +15,7 @@
 AXES = ("ctx", "head")
 LANES = 128
 EDGE = 16
-PER_STEP = 4
+PER_STEP = (8, 4, 2, 1)
 FAR = -1e30
 FRONT_STEPS = 4
 BACK_STEPS = 4
@@ -62,13 +62,13 @@
     return jnp.where(low_lanes(x.shape), swap_halves(x), y)
 
 
-def conv_rows(padded_ref, cols, kernel_ref, lengths_ref, first_row, rows, flip):
+def conv_masks(lengths_ref, first_row, rows):
     pos = first_row + lax.broadcasted_iota(jnp.int32, (rows, LANES), 0)
     start, stop = record_span(pos, lengths_ref)
-    masks = []
-    for t in range(KS):
-        at = pos + (t - HALF)
-        masks.append((at >= start) & (at < stop))
+    return [(pos + (t - HALF) >= start) & (pos + (t - HALF) < stop) for t in range(KS)]
+
+
+def conv_rows(padded_ref, cols, kernel_ref, masks, rows, flip):
     pieces = []
     for c in cols:
         lanes = pl.ds(c * LANES, LANES)
@@ -119,12 +119,11 @@
     for c in whole:
         c.wait()
     padded[pl.ds(8, rows), :] = x_ref[...].astype(F32)
-    first_row = device_index() * rows
+    masks = conv_masks(lengths_ref, device_index() * rows, rows)
     per = blk // LANES
     for step in range(FRONT_STEPS):
         mixed = conv_rows(
-            padded, range(step * per, (step + 1) * per), taps_ref, lengths_ref, first_row, rows,
-            False,
+            padded, range(step * per, (step + 1) * per), taps_ref, masks, rows, False
         ).astype(BF16)
         parts[step][0].wait()
         part = jnp.dot(mixed, w_ref[pl.ds(step * blk, blk), :], preferred_element_type=F32)
@@ -277,7 +276,7 @@
 
     def run_rest(make):
         first = groups
-        for per in (PER_STEP, 2, 1):
+        for per in PER_STEP:
             steps = (count - first) // per
             lax.fori_loop(0, steps, make(first, per), 0)
             first = first + steps * per
@@ -457,17 +456,24 @@
     edge_dkv, edge_cq = slice(2 * rows, 2 * rows + 8), slice(2 * rows + 8, 2 * rows + 16)
     pad = jnp.zeros((8, LANES), F32)
     for pair in range(heads // 2):
-        lanes = pl.ds(pair * LANES, LANES)
+        x, y = (r_ref[2 * pair + i, pl.ds(0, rows)].astype(F32) for i in range(2))
+        context[:, pl.ds(pair * LANES, LANES)] = zip_low(x, y).astype(BF16)
+    for step in range(BACK_STEPS):
+        part = pl.ds(step * blk, blk)
+        attended_ref[:, part] = jnp.dot(
+            context[...], wo_ref[:, part], preferred_element_type=F32
+        ).astype(BF16)
+    for pair in range(heads // 2):
         x, y = (r_ref[2 * pair + i].astype(F32) for i in range(2))
-        context[:, lanes] = zip_low(x[main], y[main]).astype(BF16)
 
         def gather(mix, part, edge):
             return jnp.concatenate([mix(x[part], y[part]), mix(x[edge], y[edge]), pad]).astype(BF16)
 
+        lanes = pl.ds(pair * LANES, LANES)
         grads[:, lanes] = gather(zip_high, main, edge_cq)
         grads[:, pl.ds(width + pair * LANES, LANES)] = gather(zip_low, dkv, edge_dkv)
         grads[:, pl.ds(2 * width + pair * LANES, LANES)] = gather(zip_high, dkv, edge_dkv)
-    first_row = device_index() * rows
+    masks = conv_masks(lengths_ref, device_index() * rows, rows)
     per = blk // LANES
     for step in range(BACK_STEPS):
         part = pl.ds(step * blk, blk)
@@ -478,12 +484,8 @@
         padded[pl.ds(0, 8), part] = edge
         padded[pl.ds(8, rows), part] = mixed[:rows]
         padded[pl.ds(8 + rows, 8), part] = edge
-        attended_ref[:, part] = jnp.dot(
-            context[...], wo_ref[:, part], preferred_element_type=F32
-        ).astype(BF16)
         grad_ref[:, part] = conv_rows(
-            padded, range(step * per, (step + 1) * per), taps_ref, lengths_ref, first_row, rows,
-            True,
+            padded, range(step * per, (step + 1) * per), taps_ref, masks, rows, True
         ).astype(BF16)
 
 

time: 110 us -> 107 us (0.973)
  Pallas kernels: 29.6 us -> 25.8 us
    pallas_call x1, Pallas kernels: 17 us -> 13.9 us  [attention_call(): pl.pallas_call(functools.partial(attention_kernel, pre, place), in_specs=...]
where the time goes in v4:
time: 107 us; the launch traced here: 106 us
  blocking collectives  67.8 us (63%)
  Pallas kernels  25.8 us (24%)
  starting transfers between devices  5.29 us (5%)
  waiting for transfers between devices  4.62 us (4%)
    all_to_all x2, blocking collectives, exchange(): lax.all_to_all(x, AXES, split_axis=0, concat_axis=0, axis_index_groups=sa...  67.8 us
    pallas_call x1, Pallas kernels, attention_call(): pl.pallas_call(functools.partial(attention_kernel, pre, place), in_specs=...  13.9 us
    pallas_call x1, Pallas kernels, front_call(): pl.pallas_call(front_kernel, in_specs=[smem, vmem, vmem] + [anywhere] * 5...  7.06 us
    pallas_call x1, Pallas kernels, back_call(): pl.pallas_call(back_kernel, in_specs=[smem, vmem, vmem, vmem, vmem], out_...  4.64 us
    ppermute x1, starting transfers between devices, on_device(): inner = lax.ppermute(jnp.where(even, last, first), AXES, swapped)  4.36 us
  transfers between devices with their start and end apart: 4, of which 3 were waited for; matrix products, arithmetic and copies ran while one was open for 0% of the time, Pallas kernels for 0%

profile of v4, /device:TPU:0, one launch (start us, length us, event | category | flops | bytes accessed | tf_op | source)
XLA Modules:
  0.0 105.7 jit_solution(10462226169698708208)
XLA Ops:
  0.6 0.8 broadcast_select_fusion
  1.4 0.7 collective-permute-start.1
  2.1 4.4 %collective-permute-start = (bf16[16,1024]{1,0:T(8,128)(2,1)S(1)}, bf16[16,1024]{1,0:T(8,128)(2,1)S(1)}, u32[]{:S(2)}, u32[]{:S(2)}) collective-permute-start(bf16[16,1024]{1,0:T(8,128)(2,1)S(1)} %get-tuple-element.11), channel_id=1, source_target_pairs={{0,1},{1,0},{2,3},{3,2},{4,5},{5,4},{6,7},{7,6},{8,9},{9,8},{10,11... | collective-permute-start | bytes 98312 | tf_op jit(solution)/shard_map/ppermute | solution.py:547
  6.5 0.0 collective-permute-done.1.outer_ref
  6.5 0.9 collective-permute-done.inner_ref
  7.3 0.0 copy-done.3
  7.3 0.6 copy-done.4
  7.9 7.1 %front.1 = bf16[16,256,128]{2,1,0:T(8,128)(2,1)} custom-call(s32[4]{0:T(128)} %lengths_ref.5, bf16[16,1024]{1,0:T(8,128)(2,1)} %copy-done.4, bf16[16,1024]{1,0:T(8,128)(2,1)} %copy-done.3, bf16[128,1024]{1,0:T(8,128)(2,1)} %x_hbm.1, f32[7,1024]{1,0:T(8,128)} %taps_ref.1, bf16[1024,3072]{1,0:T(8,128)(2,1)} %w_ref.1, bf16[128,1024]{1,0:T(8,128)(2,1)} %cot_hbm.1, ...), custom_call_target="tpu_custom_call" | custom-call | flops 1073741824 | bytes 8388608 | tf_op jit(solution)/shard_map/front/pallas_call | solution.py:153
  15.0 0.0 copy-start.2
  15.0 34.9 %all_to_all.10.qd_ref = bf16[16,256,128]{2,1,0:T(8,128)(2,1)S(1)} all-to-all(bf16[16,256,128]{2,1,0:T(8,128)(2,1)} %front.1), channel_id=1, replica_groups={{0,16,8,24,4,20,12,28,2,18,10,26,6,22,14,30},{1,17,9,25,5,21,13,29,3,19..., dimensions={0} | all-to-all | bytes 2097152 | tf_op jit(solution)/shard_map/all_to_all | solution.py:541
  50.0 0.0 slice-start.1
  50.0 0.1 collective-permute-start.2
  50.1 1.9 %collective-permute-done.2.kv_other = bf16[16,128,128]{2,1,0:T(8,128)(2,1)S(1)} collective-permute-done((bf16[16,128,128]{2,1,0:T(8,128)(2,1)S(1)}, bf16[16,128,128]{2,1,0:T(8,128)(2,1)S(1)}, u32[]{:S(2)}, u32[]{:S(2)}) %collective-permute-start.2) | collective-permute-done | bytes 524320 | tf_op jit(solution)/shard_map/ppermute | solution.py:556
  52.0 0.0 copy-done.2
  52.0 13.9 %attention.1 = (bf16[16,128,128]{2,1,0:T(8,128)(2,1)S(1)}, f32[16,128,128]{2,1,0:T(8,128)S(1)}, f32[16,8,128]{2,1,0:T(8,128)S(1)}, bf16[16,144,128]{2,1,0:T(8,128)(2,1)S(1)}) custom-call(s32[4]{0:T(128)S(1)} %copy-done.2, bf16[16,128,128]{2,1,0:T(8,128)(2,1)S(1)} %slice.12.kv_mine, bf16[16,128,128]{2,1,0:T(8,128)(2,1)S(1)} %collective-permute-done.2.kv_other, ...), custom_call_target="tpu_custom_call" | custom-call | flops 5368709120 | bytes 5242880 | tf_op jit(solution)/shard_map/attention/pallas_call | solution.py:365
  65.9 0.2 collective-permute-start.3
  66.1 1.9 %collective-permute-done.3.got_ref = bf16[16,144,128]{2,1,0:T(8,128)(2,1)S(1)} collective-permute-done((bf16[16,144,128]{2,1,0:T(8,128)(2,1)S(1)}, bf16[16,144,128]{2,1,0:T(8,128)(2,1)S(1)}, u32[]{:S(2)}, u32[]{:S(2)}) %collective-permute-start.3) | collective-permute-done | bytes 589856 | tf_op jit(solution)/shard_map/ppermute | solution.py:558
  67.9 0.2 combine.1
  68.1 32.9 %all_to_all.11.r_ref = bf16[16,272,128]{2,1,0:T(8,128)(2,1)S(1)} all-to-all(bf16[16,272,128]{2,1,0:T(8,128)(2,1)S(1)} %combine.1), channel_id=1, replica_groups={{0,16,8,24,4,20,12,28,2,18,10,26,6,22,14,30},{1,17,9,25,5,21,13,29,3,19..., dimensions={0} | all-to-all | bytes 2228224 | tf_op jit(solution)/shard_map/all_to_all | solution.py:541
  101.0 0.0 slice-done
  101.0 0.0 slice-done.1
  101.0 0.0 copy-done
  101.0 0.0 copy-done.1
  101.0 4.6 %back.1 = (bf16[128,1024]{1,0:T(8,128)(2,1)}, bf16[128,1024]{1,0:T(8,128)(2,1)}) custom-call(s32[4]{0:T(128)S(1)} %copy-done.2, bf16[16,272,128]{2,1,0:T(8,128)(2,1)S(1)} %all_to_all.11.r_ref, f32[7,1024]{1,0:T(8,128)S(1)} %copy-done.1, bf16[1024,3072]{1,0:T(8,128)(2,1)S(1)} %bitcast.1, bf16[1024,1024]{1,0:T(8,128)(2,1)S(1)} %copy-done), custom_call_target="tpu_custom_call" | custom-call | flops 1073741824 | bytes 8388608 | tf_op jit(solution)/shard_map/back/pallas_call | solution.py:499
  (7 shorter events, 0.0 us)
Async XLA Ops:
  1.4 5.0 %collective-permute-start.1 = (bf16[16,1024]{1,0:T(8,128)(2,1)S(1)}, bf16[16,1024]{1,0:T(8,128)(2,1)S(1)}, u32[]{:S(2)}, u32[]{:S(2)}) collective-permute-start(bf16[16,1024]{1,0:T(8,128)(2,1)S(1)} %get-tuple-element.10), channel_id=1, source_target_pairs={{1,2},{2,1},{3,4},{4,3},{5,6},{6,5},{7,8},{8,7},{9,10},{10,9},{11,... | collective-permute-start | bytes 98312 | tf_op jit(solution)/shard_map/ppermute | solution.py:548
  2.1 5.2 %collective-permute-start = (bf16[16,1024]{1,0:T(8,128)(2,1)S(1)}, bf16[16,1024]{1,0:T(8,128)(2,1)S(1)}, u32[]{:S(2)}, u32[]{:S(2)}) collective-permute-start(bf16[16,1024]{1,0:T(8,128)(2,1)S(1)} %get-tuple-element.11), channel_id=1, source_target_pairs={{0,1},{1,0},{2,3},{3,2},{4,5},{5,4},{6,7},{7,6},{8,9},{9,8},{10,11... | collective-permute-start | bytes 98312 | tf_op jit(solution)/shard_map/ppermute | solution.py:547
  6.5 0.9 copy-start.3
  7.3 0.6 copy-start.4
  15.0 37.0 %copy-start.2 = (s32[4]{0:T(128)S(1)}, s32[4]{0:T(128)}, u32[]{:S(2)}) copy-start(s32[4]{0:T(128)} %lengths_ref.5) | copy-start | bytes 52
  49.9 51.1 %slice-start = ((s8[6291456]{0:T(1024)(128)(4,1)}), s8[4194304]{0:T(1024)(128)(4,1)S(1)}, s32[]{:S(2)}) async-start(s8[6291456]{0:T(1024)(128)(4,1)} %bitcast), calls=%async_computation.2 | async-start | bytes 8388608
  50.0 51.1 %slice-start.1 = ((s8[6291456]{0:T(1024)(128)(4,1)}), s8[2097152]{0:T(1024)(128)(4,1)S(1)}, s32[]{:S(2)}) async-start(s8[6291456]{0:T(1024)(128)(4,1)} %bitcast), calls=%async_computation.3 | async-start | bytes 4194304
  50.0 2.0 %collective-permute-start.2 = (bf16[16,128,128]{2,1,0:T(8,128)(2,1)S(1)}, bf16[16,128,128]{2,1,0:T(8,128)(2,1)S(1)}, u32[]{:S(2)}, u32[]{:S(2)}) collective-permute-start(bf16[16,128,128]{2,1,0:T(8,128)(2,1)S(1)} %slice.12.kv_mine), channel_id=1, source_target_pairs={{0,1},{1,0},{2,3},{3,2},{4,5},{5,4},{6,7},{7,6},{8,9},{9,8},{10,11... | collective-permute-start | bytes 1572872 | tf_op jit(solution)/shard_map/ppermute | solution.py:556
  65.9 2.1 %collective-permute-start.3 = (bf16[16,144,128]{2,1,0:T(8,128)(2,1)S(1)}, bf16[16,144,128]{2,1,0:T(8,128)(2,1)S(1)}, u32[]{:S(2)}, u32[]{:S(2)}) collective-permute-start(bf16[16,144,128]{2,1,0:T(8,128)(2,1)S(1)} %get-tuple-element.9), channel_id=1, source_target_pairs={{0,1},{1,0},{2,3},{3,2},{4,5},{5,4},{6,7},{7,6},{8,9},{9,8},{10,11... | collective-permute-start | bytes 1769480 | tf_op jit(solution)/shard_map/ppermute | solution.py:558
  67.9 33.1 %copy-start = (bf16[1024,1024]{1,0:T(8,128)(2,1)S(1)}, bf16[1024,1024]{1,0:T(8,128)(2,1)}, u32[]{:S(2)}) copy-start(bf16[1024,1024]{1,0:T(8,128)(2,1)} %wo_ref.1) | copy-start | bytes 6291460
  67.9 33.1 %copy-start.1 = (f32[7,1024]{1,0:T(8,128)S(1)}, f32[7,1024]{1,0:T(8,128)}, u32[]{:S(2)}) copy-start(f32[7,1024]{1,0:T(8,128)} %taps_ref.1) | copy-start | bytes 86020

commit v5 on v4

--- a/solution.py
+++ b/solution.py
@@ -19,7 +19,7 @@
 FAR = -1e30
 FRONT_STEPS = 4
 BACK_STEPS = 4
-VMEM_ALL = 57_500_000
+VMEM_ALL = 55_000_000
 VMEM_MOST = 44 * 1024 * 1024
 VMEM_SOME = 24 * 1024 * 1024
 F32 = jnp.float32
@@ -191,8 +191,11 @@
     unit = HD**-0.5
     to_exp2 = unit * math.log2(math.e)
 
-    def row_at(slot, side):
-        return slot * tile + side * rows + lax.broadcasted_iota(jnp.int32, (rows, 1), 0)
+    row_in_block = lax.broadcasted_iota(jnp.int32, (rows, LANES), 0)
+
+    def recorded(slot, side, first):
+        at = first + slot * tile + side * rows
+        return (row_in_block >= starts - at) & (row_in_block < stops - at)
 
     lane = lax.broadcasted_iota(jnp.int32, (1, LANES), 1)
     starts = jnp.zeros((1, LANES), jnp.int32)
@@ -228,8 +231,7 @@
                 at = pl.ds(half * tile + i * rows, rows)
                 keys_ref[t, at] = block
                 turned_ref[t, :, at] = block.T
-                pos = origin + row_at(2 * t + i, side)
-                mark = jnp.where((pos >= starts) & (pos < stops), 0.0, FAR)
+                mark = jnp.where(recorded(2 * t + i, side, origin), 0.0, FAR)
                 marked_ref[t, at] = jnp.where(low, block.astype(F32), mark).astype(BF16)
     for t in range(pre // 2):
         acc_ref[t] = jnp.zeros_like(acc_ref[t])
@@ -239,8 +241,7 @@
             at = pl.ds(i * rows, rows)
             d_turned_ref[u, :, at] = qd.T[HD:].astype(F32)
             qd = qd.astype(F32)
-            pos = base + row_at(2 * u + i, parity)
-            mark = jnp.where((pos >= starts) & (pos < stops), 1.0, 0.0)
+            mark = jnp.where(recorded(2 * u + i, parity, base), 1.0, 0.0)
             query_ref[u, at] = jnp.where(low, qd, mark).astype(BF16)
             qd_cat_ref[u, at] = jnp.where(low, qd, 0.0).astype(BF16)
             qd_cat_ref[u, pl.ds(tile + i * rows, rows)] = jnp.where(low, 0.0, qd).astype(BF16)

time: 107 us -> 111 us (1.037)
  local copies, waits for them, and re-layouts: 0.68 us -> 3.38 us
  Pallas kernels: 25.8 us -> 28.3 us
    pallas_call x1, Pallas kernels: 13.9 us -> 16.8 us  [attention_call(): pl.pallas_call(functools.partial(attention_kernel, pre, place), in_specs=...]
    unnamed x14 -> x18, local copies, waits for them, and re-layouts: 0.64 us -> 3.34 us
where the time goes in v5:
time: 111 us; the launch traced here: 110 us
  blocking collectives  67.2 us (61%)
  Pallas kernels  28.3 us (25%)
  starting transfers between devices  5.29 us (5%)
  waiting for transfers between devices  4.63 us (4%)
  local copies, waits for them, and re-layouts  3.38 us (3%)
    all_to_all x2, blocking collectives, exchange(): lax.all_to_all(x, AXES, split_axis=0, concat_axis=0, axis_index_groups=sa...  67.2 us
    pallas_call x1, Pallas kernels, attention_call(): pl.pallas_call(functools.partial(attention_kernel, pre, place), in_specs=...  16.8 us
    pallas_call x1, Pallas kernels, front_call(): pl.pallas_call(front_kernel, in_specs=[smem, vmem, vmem] + [anywhere] * 5...  6.7 us
    pallas_call x1, Pallas kernels, back_call(): pl.pallas_call(back_kernel, in_specs=[smem, vmem, vmem, vmem, vmem], out_...  4.63 us
    ppermute x1, starting transfers between devices, on_device(): inner = lax.ppermute(jnp.where(even, last, first), AXES, swapped)  4.36 us
    unnamed x18, local copies, waits for them, and re-layouts  3.34 us
  transfers between devices with their start and end apart: 4, of which 3 were waited for; matrix products, arithmetic and copies ran while one was open for 0% of the time, Pallas kernels for 0%

profile of v5, /device:TPU:0, one launch (start us, length us, event | category | flops | bytes accessed | tf_op | source)
XLA Modules:
  0.0 110.3 jit_solution(457645543453296663)
XLA Ops:
  0.6 0.8 broadcast_select_fusion
  1.4 0.7 collective-permute-start.1
  2.1 4.4 %collective-permute-start = (bf16[16,1024]{1,0:T(8,128)(2,1)S(1)}, bf16[16,1024]{1,0:T(8,128)(2,1)S(1)}, u32[]{:S(2)}, u32[]{:S(2)}) collective-permute-start(bf16[16,1024]{1,0:T(8,128)(2,1)S(1)} %get-tuple-element.11), channel_id=1, source_target_pairs={{0,1},{1,0},{2,3},{3,2},{4,5},{5,4},{6,7},{7,6},{8,9},{9,8},{10,11... | collective-permute-start | bytes 98312 | tf_op jit(solution)/shard_map/ppermute | solution.py:548
  6.5 0.0 collective-permute-done.1.outer_ref
  6.5 0.9 collective-permute-done.inner_ref
  7.3 0.9 copy-done.1
  8.3 0.9 copy-done.2
  9.2 0.8 copy-done.3
  10.0 0.7 copy-done.5
  10.6 6.7 %front.1 = bf16[16,256,128]{2,1,0:T(8,128)(2,1)} custom-call(s32[4]{0:T(128)S(1)} %copy-done.5, bf16[16,1024]{1,0:T(8,128)(2,1)S(1)} %collective-permute-done.inner_ref, bf16[16,1024]{1,0:T(8,128)(2,1)S(1)} %collective-permute-done.1.outer_ref, bf16[128,1024]{1,0:T(8,128)(2,1)S(1)} %copy-done.1, f32[7,1024]{1,0:T(8,128)S(1)} %copy-done.3, ...), custom_call_target="tpu_custom_call" | custom-call | flops 1073741824 | bytes 8388608 | tf_op jit(solution)/shard_map/front/pallas_call | solution.py:153
  17.3 0.0 copy-start.6
  17.3 34.3 %all_to_all.10.qd_ref = bf16[16,256,128]{2,1,0:T(8,128)(2,1)S(1)} all-to-all(bf16[16,256,128]{2,1,0:T(8,128)(2,1)} %front.1), channel_id=1, replica_groups={{0,16,8,24,4,20,12,28,2,18,10,26,6,22,14,30},{1,17,9,25,5,21,13,29,3,19..., dimensions={0} | all-to-all | bytes 2097152 | tf_op jit(solution)/shard_map/all_to_all | solution.py:542
  51.7 0.0 slice-start.1
  51.7 0.1 collective-permute-start.2
  51.8 1.9 %collective-permute-done.2.kv_other = bf16[16,128,128]{2,1,0:T(8,128)(2,1)S(1)} collective-permute-done((bf16[16,128,128]{2,1,0:T(8,128)(2,1)S(1)}, bf16[16,128,128]{2,1,0:T(8,128)(2,1)S(1)}, u32[]{:S(2)}, u32[]{:S(2)}) %collective-permute-start.2) | collective-permute-done | bytes 524320 | tf_op jit(solution)/shard_map/ppermute | solution.py:557
  53.7 0.0 copy-done.6
  53.7 16.8 %attention.1 = (bf16[16,128,128]{2,1,0:T(8,128)(2,1)S(1)}, f32[16,128,128]{2,1,0:T(8,128)S(1)}, f32[16,8,128]{2,1,0:T(8,128)S(1)}, bf16[16,144,128]{2,1,0:T(8,128)(2,1)S(1)}) custom-call(s32[4]{0:T(128)S(1)} %copy-done.6, bf16[16,128,128]{2,1,0:T(8,128)(2,1)S(1)} %slice.12.kv_mine, bf16[16,128,128]{2,1,0:T(8,128)(2,1)S(1)} %collective-permute-done.2.kv_other, ...), custom_call_target="tpu_custom_call" | custom-call | flops 5368709120 | bytes 5242880 | tf_op jit(solution)/shard_map/attention/pallas_call | solution.py:366
  70.5 0.2 collective-permute-start.3
  70.7 1.9 %collective-permute-done.3.got_ref = bf16[16,144,128]{2,1,0:T(8,128)(2,1)S(1)} collective-permute-done((bf16[16,144,128]{2,1,0:T(8,128)(2,1)S(1)}, bf16[16,144,128]{2,1,0:T(8,128)(2,1)S(1)}, u32[]{:S(2)}, u32[]{:S(2)}) %collective-permute-start.3) | collective-permute-done | bytes 589856 | tf_op jit(solution)/shard_map/ppermute | solution.py:559
  72.6 0.2 combine.1
  72.8 32.9 %all_to_all.11.r_ref = bf16[16,272,128]{2,1,0:T(8,128)(2,1)S(1)} all-to-all(bf16[16,272,128]{2,1,0:T(8,128)(2,1)S(1)} %combine.1), channel_id=1, replica_groups={{0,16,8,24,4,20,12,28,2,18,10,26,6,22,14,30},{1,17,9,25,5,21,13,29,3,19..., dimensions={0} | all-to-all | bytes 2228224 | tf_op jit(solution)/shard_map/all_to_all | solution.py:542
  105.7 0.0 slice-done
  105.7 0.0 copy-done
  105.7 4.6 %back.1 = (bf16[128,1024]{1,0:T(8,128)(2,1)}, bf16[128,1024]{1,0:T(8,128)(2,1)}) custom-call(s32[4]{0:T(128)S(1)} %copy-done.6, bf16[16,272,128]{2,1,0:T(8,128)(2,1)S(1)} %all_to_all.11.r_ref, f32[7,1024]{1,0:T(8,128)S(1)} %copy-done.4, bf16[1024,3072]{1,0:T(8,128)(2,1)S(1)} %bitcast.1, bf16[1024,1024]{1,0:T(8,128)(2,1)S(1)} %copy-done), custom_call_target="tpu_custom_call" | custom-call | flops 1073741824 | bytes 8388608 | tf_op jit(solution)/shard_map/back/pallas_call | solution.py:500
  (11 shorter events, 0.1 us)
Async XLA Ops:
  1.4 5.0 %collective-permute-start.1 = (bf16[16,1024]{1,0:T(8,128)(2,1)S(1)}, bf16[16,1024]{1,0:T(8,128)(2,1)S(1)}, u32[]{:S(2)}, u32[]{:S(2)}) collective-permute-start(bf16[16,1024]{1,0:T(8,128)(2,1)S(1)} %get-tuple-element.10), channel_id=1, source_target_pairs={{1,2},{2,1},{3,4},{4,3},{5,6},{6,5},{7,8},{8,7},{9,10},{10,9},{11,... | collective-permute-start | bytes 98312 | tf_op jit(solution)/shard_map/ppermute | solution.py:549
  2.1 5.2 %collective-permute-start = (bf16[16,1024]{1,0:T(8,128)(2,1)S(1)}, bf16[16,1024]{1,0:T(8,128)(2,1)S(1)}, u32[]{:S(2)}, u32[]{:S(2)}) collective-permute-start(bf16[16,1024]{1,0:T(8,128)(2,1)S(1)} %get-tuple-element.11), channel_id=1, source_target_pairs={{0,1},{1,0},{2,3},{3,2},{4,5},{5,4},{6,7},{7,6},{8,9},{9,8},{10,11... | collective-permute-start | bytes 98312 | tf_op jit(solution)/shard_map/ppermute | solution.py:548
  7.3 0.9 copy-start.1
  8.3 0.9 copy-start.2
  9.2 0.8 copy-start.3
  10.0 0.7 copy-start.5
  17.3 36.3 %copy-start.6 = (s32[4]{0:T(128)S(1)}, s32[4]{0:T(128)}, u32[]{:S(2)}) copy-start(s32[4]{0:T(128)} %lengths_ref.5) | copy-start | bytes 52
  51.6 54.0 %slice-start = ((s8[6291456]{0:T(1024)(128)(4,1)}), s8[4194304]{0:T(1024)(128)(4,1)S(1)}, s32[]{:S(2)}) async-start(s8[6291456]{0:T(1024)(128)(4,1)} %bitcast), calls=%async_computation.2 | async-start | bytes 8388608
  51.7 54.0 %slice-start.1 = ((s8[6291456]{0:T(1024)(128)(4,1)}), s8[2097152]{0:T(1024)(128)(4,1)S(1)}, s32[]{:S(2)}) async-start(s8[6291456]{0:T(1024)(128)(4,1)} %bitcast), calls=%async_computation.3 | async-start | bytes 4194304
  51.7 2.0 %collective-permute-start.2 = (bf16[16,128,128]{2,1,0:T(8,128)(2,1)S(1)}, bf16[16,128,128]{2,1,0:T(8,128)(2,1)S(1)}, u32[]{:S(2)}, u32[]{:S(2)}) collective-permute-start(bf16[16,128,128]{2,1,0:T(8,128)(2,1)S(1)} %slice.12.kv_mine), channel_id=1, source_target_pairs={{0,1},{1,0},{2,3},{3,2},{4,5},{5,4},{6,7},{7,6},{8,9},{9,8},{10,11... | collective-permute-start | bytes 1572872 | tf_op jit(solution)/shard_map/ppermute | solution.py:557
  70.5 2.1 %collective-permute-start.3 = (bf16[16,144,128]{2,1,0:T(8,128)(2,1)S(1)}, bf16[16,144,128]{2,1,0:T(8,128)(2,1)S(1)}, u32[]{:S(2)}, u32[]{:S(2)}) collective-permute-start(bf16[16,144,128]{2,1,0:T(8,128)(2,1)S(1)} %get-tuple-element.9), channel_id=1, source_target_pairs={{0,1},{1,0},{2,3},{3,2},{4,5},{5,4},{6,7},{7,6},{8,9},{9,8},{10,11... | collective-permute-start | bytes 1769480 | tf_op jit(solution)/shard_map/ppermute | solution.py:559
  72.6 33.1 %copy-start = (bf16[1024,1024]{1,0:T(8,128)(2,1)S(1)}, bf16[1024,1024]{1,0:T(8,128)(2,1)}, u32[]{:S(2)}) copy-start(bf16[1024,1024]{1,0:T(8,128)(2,1)} %wo_ref.1) | copy-start | bytes 6291460
  72.6 33.1 %copy-start.4 = (f32[7,1024]{1,0:T(8,128)S(1)}, f32[7,1024]{1,0:T(8,128)}, u32[]{:S(2)}) copy-start(f32[7,1024]{1,0:T(8,128)} %taps_ref.1) | copy-start | bytes 86020

commit v6 on v5

--- a/solution.py
+++ b/solution.py
@@ -19,7 +19,7 @@
 FAR = -1e30
 FRONT_STEPS = 4
 BACK_STEPS = 4
-VMEM_ALL = 55_000_000
+VMEM_ALL = 57_500_000
 VMEM_MOST = 44 * 1024 * 1024
 VMEM_SOME = 24 * 1024 * 1024
 F32 = jnp.float32
@@ -116,7 +116,7 @@
     inner, outer = inner_ref[...].astype(F32), outer_ref[...].astype(F32)
     padded[pl.ds(0, 8), :] = jnp.where(even, outer[EDGE - 8 :], inner[EDGE - 8 :])
     padded[pl.ds(8 + rows, 8), :] = jnp.where(even, inner[:8], outer[:8])
-    for c in whole:
+    for c in whole[:2]:
         c.wait()
     padded[pl.ds(8, rows), :] = x_ref[...].astype(F32)
     masks = conv_masks(lengths_ref, device_index() * rows, rows)
@@ -131,6 +131,8 @@
             projected[...] = part
         else:
             projected[...] += part
+        if step == 0:
+            whole[2].wait()
         parts[step][1].wait()
         d_rows[:, pl.ds(step * blk, blk)] = lax.dot_general(
             cot_ref[...], wo_ref[pl.ds(step * blk, blk), :], (((1,), (1,)), ((), ())),

time: 111 us -> 108 us (0.973); the launches traced: 110 us -> 109 us
  local copies, waits for them, and re-layouts: 3.38 us -> 0.68 us
    unnamed x18 -> x14, local copies, waits for them, and re-layouts: 3.34 us -> 0.64 us
where the time goes in v6:
time: 108 us; the launch traced here: 109 us
  blocking collectives  67.8 us (63%)
  Pallas kernels  28.7 us (27%)
  starting transfers between devices  5.29 us (5%)
  waiting for transfers between devices  4.63 us (4%)
    all_to_all x2, blocking collectives, exchange(): lax.all_to_all(x, AXES, split_axis=0, concat_axis=0, axis_index_groups=sa...  67.8 us
    pallas_call x1, Pallas kernels, attention_call(): pl.pallas_call(functools.partial(attention_kernel, pre, place), in_specs=...  16.8 us
    pallas_call x1, Pallas kernels, front_call(): pl.pallas_call(front_kernel, in_specs=[smem, vmem, vmem] + [anywhere] * 5...  7.07 us
    pallas_call x1, Pallas kernels, back_call(): pl.pallas_call(back_kernel, in_specs=[smem, vmem, vmem, vmem, vmem], out_...  4.63 us
    ppermute x1, starting transfers between devices, on_device(): inner = lax.ppermute(jnp.where(even, last, first), AXES, swapped)  4.36 us
  transfers between devices with their start and end apart: 4, of which 3 were waited for; matrix products, arithmetic and copies ran while one was open for 0% of the time, Pallas kernels for 0%

profile of v6, /device:TPU:0, one launch (start us, length us, event | category | flops | bytes accessed | tf_op | source)
XLA Modules:
  0.0 108.6 jit_solution(4677489249212499573)
XLA Ops:
  0.6 0.8 broadcast_select_fusion
  1.4 0.7 collective-permute-start.1
  2.1 4.4 %collective-permute-start = (bf16[16,1024]{1,0:T(8,128)(2,1)S(1)}, bf16[16,1024]{1,0:T(8,128)(2,1)S(1)}, u32[]{:S(2)}, u32[]{:S(2)}) collective-permute-start(bf16[16,1024]{1,0:T(8,128)(2,1)S(1)} %get-tuple-element.11), channel_id=1, source_target_pairs={{0,1},{1,0},{2,3},{3,2},{4,5},{5,4},{6,7},{7,6},{8,9},{9,8},{10,11... | collective-permute-start | bytes 98312 | tf_op jit(solution)/shard_map/ppermute | solution.py:550
  6.5 0.0 collective-permute-done.1.outer_ref
  6.5 0.9 collective-permute-done.inner_ref
  7.3 0.0 copy-done.3
  7.3 0.6 copy-done.4
  7.9 7.1 %front.1 = bf16[16,256,128]{2,1,0:T(8,128)(2,1)} custom-call(s32[4]{0:T(128)} %lengths_ref.5, bf16[16,1024]{1,0:T(8,128)(2,1)} %copy-done.4, bf16[16,1024]{1,0:T(8,128)(2,1)} %copy-done.3, bf16[128,1024]{1,0:T(8,128)(2,1)} %x_hbm.1, f32[7,1024]{1,0:T(8,128)} %taps_ref.1, bf16[1024,3072]{1,0:T(8,128)(2,1)} %w_ref.1, bf16[128,1024]{1,0:T(8,128)(2,1)} %cot_hbm.1, ...), custom_call_target="tpu_custom_call" | custom-call | flops 1073741824 | bytes 8388608 | tf_op jit(solution)/shard_map/front/pallas_call | solution.py:155
  15.0 0.0 copy-start.2
  15.0 34.9 %all_to_all.10.qd_ref = bf16[16,256,128]{2,1,0:T(8,128)(2,1)S(1)} all-to-all(bf16[16,256,128]{2,1,0:T(8,128)(2,1)} %front.1), channel_id=1, replica_groups={{0,16,8,24,4,20,12,28,2,18,10,26,6,22,14,30},{1,17,9,25,5,21,13,29,3,19..., dimensions={0} | all-to-all | bytes 2097152 | tf_op jit(solution)/shard_map/all_to_all | solution.py:544
  50.0 0.0 slice-start.1
  50.0 0.1 collective-permute-start.2
  50.0 1.9 %collective-permute-done.2.kv_other = bf16[16,128,128]{2,1,0:T(8,128)(2,1)S(1)} collective-permute-done((bf16[16,128,128]{2,1,0:T(8,128)(2,1)S(1)}, bf16[16,128,128]{2,1,0:T(8,128)(2,1)S(1)}, u32[]{:S(2)}, u32[]{:S(2)}) %collective-permute-start.2) | collective-permute-done | bytes 524320 | tf_op jit(solution)/shard_map/ppermute | solution.py:559
  51.9 0.0 copy-done.2
  51.9 16.8 %attention.1 = (bf16[16,128,128]{2,1,0:T(8,128)(2,1)S(1)}, f32[16,128,128]{2,1,0:T(8,128)S(1)}, f32[16,8,128]{2,1,0:T(8,128)S(1)}, bf16[16,144,128]{2,1,0:T(8,128)(2,1)S(1)}) custom-call(s32[4]{0:T(128)S(1)} %copy-done.2, bf16[16,128,128]{2,1,0:T(8,128)(2,1)S(1)} %slice.12.kv_mine, bf16[16,128,128]{2,1,0:T(8,128)(2,1)S(1)} %collective-permute-done.2.kv_other, ...), custom_call_target="tpu_custom_call" | custom-call | flops 5368709120 | bytes 5242880 | tf_op jit(solution)/shard_map/attention/pallas_call | solution.py:368
  68.8 0.2 collective-permute-start.3
  69.0 1.9 %collective-permute-done.3.got_ref = bf16[16,144,128]{2,1,0:T(8,128)(2,1)S(1)} collective-permute-done((bf16[16,144,128]{2,1,0:T(8,128)(2,1)S(1)}, bf16[16,144,128]{2,1,0:T(8,128)(2,1)S(1)}, u32[]{:S(2)}, u32[]{:S(2)}) %collective-permute-start.3) | collective-permute-done | bytes 589856 | tf_op jit(solution)/shard_map/ppermute | solution.py:561
  70.9 0.2 combine.1
  71.0 32.9 %all_to_all.11.r_ref = bf16[16,272,128]{2,1,0:T(8,128)(2,1)S(1)} all-to-all(bf16[16,272,128]{2,1,0:T(8,128)(2,1)S(1)} %combine.1), channel_id=1, replica_groups={{0,16,8,24,4,20,12,28,2,18,10,26,6,22,14,30},{1,17,9,25,5,21,13,29,3,19..., dimensions={0} | all-to-all | bytes 2228224 | tf_op jit(solution)/shard_map/all_to_all | solution.py:544
  103.9 0.0 slice-done
  103.9 0.0 slice-done.1
  103.9 0.0 copy-done
  103.9 0.0 copy-done.1
  104.0 4.6 %back.1 = (bf16[128,1024]{1,0:T(8,128)(2,1)}, bf16[128,1024]{1,0:T(8,128)(2,1)}) custom-call(s32[4]{0:T(128)S(1)} %copy-done.2, bf16[16,272,128]{2,1,0:T(8,128)(2,1)S(1)} %all_to_all.11.r_ref, f32[7,1024]{1,0:T(8,128)S(1)} %copy-done.1, bf16[1024,3072]{1,0:T(8,128)(2,1)S(1)} %bitcast.1, bf16[1024,1024]{1,0:T(8,128)(2,1)S(1)} %copy-done), custom_call_target="tpu_custom_call" | custom-call | flops 1073741824 | bytes 8388608 | tf_op jit(solution)/shard_map/back/pallas_call | solution.py:502
  (7 shorter events, 0.0 us)
Async XLA Ops:
  1.4 5.0 %collective-permute-start.1 = (bf16[16,1024]{1,0:T(8,128)(2,1)S(1)}, bf16[16,1024]{1,0:T(8,128)(2,1)S(1)}, u32[]{:S(2)}, u32[]{:S(2)}) collective-permute-start(bf16[16,1024]{1,0:T(8,128)(2,1)S(1)} %get-tuple-element.10), channel_id=1, source_target_pairs={{1,2},{2,1},{3,4},{4,3},{5,6},{6,5},{7,8},{8,7},{9,10},{10,9},{11,... | collective-permute-start | bytes 98312 | tf_op jit(solution)/shard_map/ppermute | solution.py:551
  2.1 5.2 %collective-permute-start = (bf16[16,1024]{1,0:T(8,128)(2,1)S(1)}, bf16[16,1024]{1,0:T(8,128)(2,1)S(1)}, u32[]{:S(2)}, u32[]{:S(2)}) collective-permute-start(bf16[16,1024]{1,0:T(8,128)(2,1)S(1)} %get-tuple-element.11), channel_id=1, source_target_pairs={{0,1},{1,0},{2,3},{3,2},{4,5},{5,4},{6,7},{7,6},{8,9},{9,8},{10,11... | collective-permute-start | bytes 98312 | tf_op jit(solution)/shard_map/ppermute | solution.py:550
  6.5 0.9 copy-start.3
  7.3 0.6 copy-start.4
  15.0 36.9 %copy-start.2 = (s32[4]{0:T(128)S(1)}, s32[4]{0:T(128)}, u32[]{:S(2)}) copy-start(s32[4]{0:T(128)} %lengths_ref.5) | copy-start | bytes 52
  49.9 54.0 %slice-start = ((s8[6291456]{0:T(1024)(128)(4,1)}), s8[4194304]{0:T(1024)(128)(4,1)S(1)}, s32[]{:S(2)}) async-start(s8[6291456]{0:T(1024)(128)(4,1)} %bitcast), calls=%async_computation.2 | async-start | bytes 8388608
  50.0 54.0 %slice-start.1 = ((s8[6291456]{0:T(1024)(128)(4,1)}), s8[2097152]{0:T(1024)(128)(4,1)S(1)}, s32[]{:S(2)}) async-start(s8[6291456]{0:T(1024)(128)(4,1)} %bitcast), calls=%async_computation.3 | async-start | bytes 4194304
  50.0 2.0 %collective-permute-start.2 = (bf16[16,128,128]{2,1,0:T(8,128)(2,1)S(1)}, bf16[16,128,128]{2,1,0:T(8,128)(2,1)S(1)}, u32[]{:S(2)}, u32[]{:S(2)}) collective-permute-start(bf16[16,128,128]{2,1,0:T(8,128)(2,1)S(1)} %slice.12.kv_mine), channel_id=1, source_target_pairs={{0,1},{1,0},{2,3},{3,2},{4,5},{5,4},{6,7},{7,6},{8,9},{9,8},{10,11... | collective-permute-start | bytes 1572872 | tf_op jit(solution)/shard_map/ppermute | solution.py:559
  68.8 2.1 %collective-permute-start.3 = (bf16[16,144,128]{2,1,0:T(8,128)(2,1)S(1)}, bf16[16,144,128]{2,1,0:T(8,128)(2,1)S(1)}, u32[]{:S(2)}, u32[]{:S(2)}) collective-permute-start(bf16[16,144,128]{2,1,0:T(8,128)(2,1)S(1)} %get-tuple-element.9), channel_id=1, source_target_pairs={{0,1},{1,0},{2,3},{3,2},{4,5},{5,4},{6,7},{7,6},{8,9},{9,8},{10,11... | collective-permute-start | bytes 1769480 | tf_op jit(solution)/shard_map/ppermute | solution.py:561
  70.9 33.1 %copy-start = (bf16[1024,1024]{1,0:T(8,128)(2,1)S(1)}, bf16[1024,1024]{1,0:T(8,128)(2,1)}, u32[]{:S(2)}) copy-start(bf16[1024,1024]{1,0:T(8,128)(2,1)} %wo_ref.1) | copy-start | bytes 6291460
  70.9 33.1 %copy-start.1 = (f32[7,1024]{1,0:T(8,128)S(1)}, f32[7,1024]{1,0:T(8,128)}, u32[]{:S(2)}) copy-start(f32[7,1024]{1,0:T(8,128)} %taps_ref.1) | copy-start | bytes 86020
